TPU v7x, 32 devices: a whole 2x2x4 slice. The times are simulated.
32 devices in a mesh: section: 2 (over core), group: 4 (over y, x), replica: 4 (over z).
Axes of the slice: x: 2, y: 2, z: 4, core: 2. Of those that a mesh axis runs over, the one named last changes fastest.
Arguments:
- tokens: bfloat16 [2, 4096, 768], P(None, ('group', 'replica')), may hold values from -6 to 6
- out_grad: bfloat16 [2, 4096, 768], P(None, ('group', 'replica')), may hold values from -6 to 6
- doc_lengths: int32 [2, 4, 8], P(None, 'group'), may hold values from 1 to 512, 1024 in all within a row
- norm_gain: bfloat16 [2, 768], P('section', 'group'), may hold values from 0.5 to 1.5
- in_weight: bfloat16 [2, 768, 3352], P('section', 'group'), may hold values from -0.21875 to 0.21875
- conv_weight: bfloat16 [2, 1792, 4], P('section', 'group'), may hold values from -3 to 3
- conv_bias: bfloat16 [2, 1792], P('section', 'group'), may hold values from -3 to 3
- dt_bias: bfloat16 [2, 24], P('section', 'group'), may hold values from -7 to -2
- a_log: bfloat16 [2, 24], P('section', 'group'), may hold values from -4.59375 to 0.69921875
- skip_gain: bfloat16 [2, 24], P('section', 'group'), may hold values from 0.5 to 1.5
- out_norm_gain: bfloat16 [2, 1536], P('section', 'group'), may hold values from 0.5 to 1.5
- out_weight: bfloat16 [2, 1536, 768], P('section', 'group'), may hold values from -0.15625 to 0.15625
Outputs:
- section_out: bfloat16 [2, 2, 4096, 768], P('section', None, ('group', 'replica'))
- section_in_grad: float32 [2, 2, 4096, 768], P('section', None, ('group', 'replica'))
- grad_norm_gain: float32 [2, 768], P('section', 'group')
- grad_in_weight: float32 [2, 768, 3352], P('section', 'group')
- grad_conv_weight: float32 [2, 1792, 4], P('section', 'group')
- grad_conv_bias: float32 [2, 1792], P('section', 'group')
- grad_dt_bias: float32 [2, 24], P('section', 'group')
- grad_a_log: float32 [2, 24], P('section', 'group')
- grad_skip_gain: float32 [2, 24], P('section', 'group')
- grad_out_norm_gain: float32 [2, 1536], P('section', 'group')
- grad_out_weight: float32 [2, 1536, 768], P('section', 'group')
Inputs may be any that keep to these rules, and one draw needn't show every extreme that they name: `doc_lengths`: each row of 8 lengths sums to 1024; the largest in every row is exactly 512.
All inputs are finite; a program needn't handle non-finite values.
Results may differ from a plain program's by a relative error of at most 0.0094.
Values may be sent and summed in bfloat16 or wider, within the bound.
A program may use at most 256 MiB of HBM per device.

v0:
```python
import jax
import jax.numpy as jnp
from jax import lax
from jax.sharding import PartitionSpec as P

H = 24
P_SIZE = 64
N = 128
KW = 4
SPAN = 256
INNER = 1536
CONVDIM = 1792


EPSILON = 1e-05
PRECISE = lax.Precision.HIGHEST


def passed_along(block, axis, distance):
    devices = range(lax.axis_size(axis))
    route = [(i - distance, i) for i in devices if i - distance in devices]
    return lax.ppermute(block, axis, route)


def prefix(part, axis, combine, identity, reverse):
    count = lax.axis_size(axis)
    place = lax.axis_index(axis)
    ahead = count - 1 - place if reverse else place
    gathered = jax.tree.map(lambda a: lax.all_gather(a, axis), part)
    state = jax.tree.map(lambda a, e: jnp.zeros_like(a) + jnp.asarray(e, a.dtype), part, identity)

    def one(hop, state):
        source = count - 1 - hop if reverse else hop
        return combine(
            state, jax.tree.map(lambda a: lax.dynamic_index_in_dim(a, source, 0, False), gathered)
        )

    return lax.fori_loop(0, ahead, one, state)


def doc_index(lengths_row, first_pos, count_rows):
    position = first_pos + jnp.arange(count_rows, dtype=jnp.int32)
    ends_cum = jnp.cumsum(lengths_row)
    counted = jnp.sum((ends_cum[None, :] <= position[:, None]).astype(jnp.int32), axis=1)
    return jnp.where(position < 0, -1, counted)


def block_step(memory, block_data):
    inputs, in_basis, out_basis, step_size, log_decay, doc_rows, before = block_data
    length = doc_rows.shape[0]
    cumulate = jnp.cumsum(log_decay, axis=0)
    order_idx = jnp.arange(length)
    allowed = (doc_rows[:, None] == doc_rows[None, :]) & (order_idx[:, None] >= order_idx[None, :])
    by_head = cumulate.T
    spread_log = by_head[:, :, None] - by_head[:, None, :]
    decay_mat = jnp.where(allowed[None], jnp.exp(jnp.where(allowed[None], spread_log, 0.0)), 0.0)
    inner_cb = jnp.dot(out_basis, in_basis.T, precision=PRECISE)
    weight_mat = decay_mat * inner_cb[None] * step_size.T[:, None, :]
    intra_out = jnp.einsum("hts,shp->thp", weight_mat, inputs, precision=PRECISE)
    inflow = (doc_rows == before).astype(jnp.float32)
    inter_out = (jnp.exp(cumulate) * inflow[:, None])[:, :, None] * jnp.einsum(
        "tn,hpn->thp", out_basis, memory, precision=PRECISE
    )
    last_doc = doc_rows[-1]
    tail_weight = (
        jnp.exp(cumulate[-1][None, :] - cumulate)
        * (doc_rows == last_doc).astype(jnp.float32)[:, None]
        * step_size
    )
    fresh_state = jnp.einsum(
        "shp,sn->hpn", tail_weight[:, :, None] * inputs, in_basis, precision=PRECISE
    )
    carry_scale = (jnp.exp(cumulate[-1]) * (last_doc == before).astype(jnp.float32))[:, None, None]
    return (memory * carry_scale + fresh_state, intra_out + inter_out)


def local_mixer(extended, dt_raw, conv_taps, conv_shift, dt_shift, log_rate, skip_part, doc_ext):
    row_count = dt_raw.shape[0]
    doc_rows = doc_ext[KW - 1 :]
    conv_sum = conv_shift[None, :]
    for offset in range(KW):
        same_doc = (doc_ext[offset : offset + row_count] == doc_rows).astype(jnp.float32)
        conv_sum = (
            conv_sum
            + conv_taps[:, offset][None, :]
            * extended[offset : offset + row_count]
            * same_doc[:, None]
        )
    activated = jax.nn.silu(conv_sum)
    inputs = activated[:, :INNER].reshape(row_count, H, P_SIZE)
    in_basis = activated[:, INNER : INNER + N]
    out_basis = activated[:, INNER + N :]
    step_size = jax.nn.softplus(dt_raw + dt_shift[None, :])
    log_decay = -step_size * jnp.exp(log_rate)[None, :]
    before_dev = doc_ext[KW - 2]
    blocks_num = row_count // SPAN
    befores = jnp.concatenate([before_dev[None], doc_rows[SPAN - 1 :: SPAN][:-1]], axis=0)
    block_data = (
        inputs.reshape(blocks_num, SPAN, H, P_SIZE),
        in_basis.reshape(blocks_num, SPAN, N),
        out_basis.reshape(blocks_num, SPAN, N),
        step_size.reshape(blocks_num, SPAN, H),
        log_decay.reshape(blocks_num, SPAN, H),
        doc_rows.reshape(blocks_num, SPAN),
        befores,
    )
    end_state, block_out = lax.scan(
        jax.checkpoint(block_step), jnp.zeros((H, P_SIZE, N), jnp.float32), block_data
    )
    cumulate = jnp.cumsum(log_decay, axis=0)
    inflow = (doc_rows == before_dev).astype(jnp.float32)
    weight_in = jnp.exp(cumulate) * inflow[:, None]
    pass_on = jnp.exp(cumulate[-1]) * (doc_rows[-1] == before_dev).astype(jnp.float32)
    mixed_loc = block_out.reshape(row_count, H, P_SIZE) + skip_part[None, :, None] * inputs
    return (mixed_loc, out_basis, weight_in, end_state, pass_on)


def gated_norm(mixed_loc, out_basis, weight_in, entering, gate_raw, out_gain):
    row_count = gate_raw.shape[0]
    summed = mixed_loc + weight_in[:, :, None] * jnp.einsum(
        "tn,hpn->thp", out_basis, entering, precision=PRECISE
    )
    flat_out = summed.reshape(row_count, INNER)
    gated_out = flat_out * jax.nn.silu(gate_raw)
    return (
        gated_out
        * lax.rsqrt(jnp.mean(gated_out * gated_out, axis=-1, keepdims=True) + EPSILON)
        * out_gain[None, :]
    )


def rms_scale(values, gain_vec):
    return (
        values
        * lax.rsqrt(jnp.mean(values * values, axis=-1, keepdims=True) + EPSILON)
        * gain_vec[None, :]
    )


def join_linear(earlier, later):
    return (earlier[0] * later[0], later[0][:, None, None] * earlier[1] + later[1])


def on_device(
    tokens,
    out_grad,
    doc_lengths,
    norm_gain,
    in_weight,
    conv_weight,
    conv_bias,
    dt_bias,
    a_log,
    skip_gain,
    out_norm_gain,
    out_weight,
):
    micro_count = tokens.shape[0]
    row_count = tokens.shape[1]
    model_width = tokens.shape[2]
    section_idx = lax.axis_index("section")
    at_first = section_idx == 0
    replica_idx = lax.axis_index("replica")
    first_pos = replica_idx * row_count - (KW - 1)
    group_count = lax.axis_size("group")
    shards = (
        norm_gain[0],
        in_weight[0],
        conv_weight[0],
        conv_bias[0],
        dt_bias[0],
        a_log[0],
        skip_gain[0],
        out_norm_gain[0],
        out_weight[0],
    )
    identity_pair = (jnp.ones((H,), jnp.float32), jnp.zeros((H, P_SIZE, N), jnp.float32))

    def collect():
        return (
            lax.all_gather(shards[0], "group", axis=0, tiled=True),
            lax.all_gather(shards[1], "group", axis=0, tiled=True),
            lax.all_gather(shards[2], "group", axis=0, tiled=True),
            lax.all_gather(shards[3], "group", axis=0, tiled=True),
            lax.all_gather(shards[4], "group", axis=0, tiled=True),
            lax.all_gather(shards[5], "group", axis=0, tiled=True),
            lax.all_gather(shards[6], "group", axis=0, tiled=True),
            lax.all_gather(shards[7], "group", axis=0, tiled=True),
            lax.all_gather(shards[8], "group", axis=0, tiled=True),
        )

    def doc_ext_for(batch_idx):
        lengths_row = lax.dynamic_index_in_dim(doc_lengths[:, 0, :], batch_idx, 0, keepdims=False)
        return doc_index(lengths_row, first_pos, row_count + KW - 1)

    def small_params(params_full):
        return tuple((param_item.astype(jnp.float32) for param_item in params_full[2:7]))

    def backward_layer(
        incoming, layer_in, params_full, doc_ext, normed, projected, extended, entering
    ):
        values = layer_in.astype(jnp.float32)
        mixer_out, mixer_back = jax.vjp(
            lambda ext_arg, dt_arg, taps_arg, shift_arg, bias_arg, rate_arg, skip_arg: local_mixer(
                ext_arg, dt_arg, taps_arg, shift_arg, bias_arg, rate_arg, skip_arg, doc_ext
            ),
            extended,
            projected[:, INNER + CONVDIM :],
            *small_params(params_full)
        )
        result, tail_back = jax.vjp(
            gated_norm,
            mixer_out[0],
            mixer_out[1],
            mixer_out[2],
            entering,
            projected[:, :INNER],
            params_full[7].astype(jnp.float32),
        )
        result_low = result.astype(jnp.bfloat16)
        grad_out_weight = jnp.dot(result_low.T, incoming, preferred_element_type=jnp.float32)
        grad_result = jnp.dot(incoming, params_full[8].T, preferred_element_type=jnp.float32)
        grad_mixed, grad_basis, grad_weight_in, grad_entering, grad_gate, grad_gain_out = tail_back(
            grad_result
        )
        carried = prefix(
            (mixer_out[4], grad_entering), "replica", join_linear, identity_pair, True
        )[1]
        grad_pass = jnp.sum(carried * entering, axis=(1, 2))
        grad_ext, grad_dt, grad_taps, grad_shift, grad_bias, grad_rate, grad_skip = mixer_back(
            (grad_mixed, grad_basis, grad_weight_in, carried, grad_pass)
        )
        rim_back = passed_along(grad_ext[: KW - 1], "replica", -1)
        grad_conv = grad_ext[KW - 1 :]
        grad_conv = jnp.concatenate(
            [grad_conv[: row_count - (KW - 1)], grad_conv[row_count - (KW - 1) :] + rim_back],
            axis=0,
        )
        grad_proj = jnp.concatenate([grad_gate, grad_conv, grad_dt], axis=1).astype(jnp.bfloat16)
        grad_in_weight = jnp.dot(normed.T, grad_proj, preferred_element_type=jnp.float32)
        grad_normed = jnp.dot(grad_proj, params_full[1].T, preferred_element_type=jnp.float32)
        unused_norm, norm_back = jax.vjp(rms_scale, values, params_full[0].astype(jnp.float32))
        grad_values, grad_gain_in = norm_back(grad_normed)
        grad_input = incoming.astype(jnp.float32) + grad_values
        return (
            grad_input,
            (
                grad_gain_in,
                grad_in_weight,
                grad_taps,
                grad_shift,
                grad_bias,
                grad_rate,
                grad_skip,
                grad_gain_out,
                grad_out_weight,
            ),
        )

    sent_rows = jnp.zeros((row_count, model_width), jnp.bfloat16)
    out_buf = jnp.zeros((micro_count, row_count, model_width), jnp.bfloat16)
    input_list = []
    saved_list = []
    for tick_num in range(micro_count + 1):
        received = passed_along(sent_rows, "section", 1)
        batch_idx = jnp.clip(tick_num - section_idx, 0, micro_count - 1)
        is_valid = (tick_num - section_idx >= 0) & (tick_num - section_idx < micro_count)
        own_tokens = lax.dynamic_index_in_dim(tokens, batch_idx, 0, keepdims=False)
        layer_in = jnp.where(at_first, own_tokens, received)
        params_full = collect()
        doc_ext = doc_ext_for(batch_idx)
        prepare_values = layer_in.astype(jnp.float32)
        prepare_normed = rms_scale(prepare_values, params_full[0].astype(jnp.float32)).astype(
            jnp.bfloat16
        )
        prepare_projected = jnp.dot(
            prepare_normed, params_full[1], preferred_element_type=jnp.float32
        )
        conv_raw = prepare_projected[:, INNER : INNER + CONVDIM]
        rim_rows = passed_along(conv_raw[row_count - (KW - 1) :], "replica", 1)
        prepare_extended = jnp.concatenate([rim_rows, conv_raw], axis=0)
        prepare_mixer_out = local_mixer(
            prepare_extended,
            prepare_projected[:, INNER + CONVDIM :],
            *small_params(params_full),
            doc_ext
        )
        prepare_entering = prefix(
            (prepare_mixer_out[4], prepare_mixer_out[3]),
            "replica",
            join_linear,
            identity_pair,
            False,
        )[1]
        normed = prepare_normed
        projected = prepare_projected
        extended = prepare_extended
        entering = prepare_entering
        mixer_out = prepare_mixer_out
        result = gated_norm(
            mixer_out[0],
            mixer_out[1],
            mixer_out[2],
            entering,
            projected[:, :INNER],
            params_full[7].astype(jnp.float32),
        )
        output = (
            layer_in.astype(jnp.float32)
            + jnp.dot(
                result.astype(jnp.bfloat16), params_full[8], preferred_element_type=jnp.float32
            )
        ).astype(jnp.bfloat16)
        current = lax.dynamic_index_in_dim(out_buf, batch_idx, 0, keepdims=False)
        out_buf = lax.dynamic_update_index_in_dim(
            out_buf, jnp.where(is_valid, output, current), batch_idx, 0
        )
        sent_rows = output
        input_list.append(layer_in)
        saved_list.append((normed, projected, extended, entering))
    stacked_in = jnp.stack(input_list)
    stacked_saved = jax.tree.map(lambda *stack_items: jnp.stack(stack_items), *saved_list)
    grad_acc = tuple(
        (
            jnp.zeros((shard_item.shape[0] * group_count,) + shard_item.shape[1:], jnp.float32)
            for shard_item in shards
        )
    )
    back_rows = jnp.zeros((row_count, model_width), jnp.bfloat16)
    grad_buf = jnp.zeros((micro_count, row_count, model_width), jnp.float32)
    for tick_num in range(micro_count + 1):
        received = passed_along(back_rows, "section", -1)
        batch_raw = tick_num - 1 + section_idx
        batch_idx = jnp.clip(batch_raw, 0, micro_count - 1)
        is_valid = (batch_raw >= 0) & (batch_raw < micro_count)
        fwd_tick = jnp.clip(tick_num - 1 + 2 * section_idx, 0, micro_count)
        own_grad = lax.dynamic_index_in_dim(out_grad, batch_idx, 0, keepdims=False)
        incoming = jnp.where(at_first, received, own_grad)
        params_full = collect()
        doc_ext = doc_ext_for(batch_idx)
        layer_in = lax.dynamic_index_in_dim(stacked_in, fwd_tick, 0, keepdims=False)
        normed, projected, extended, entering = jax.tree.map(
            lambda stack_arr: lax.dynamic_index_in_dim(stack_arr, fwd_tick, 0, keepdims=False),
            stacked_saved,
        )
        grad_input, layer_grads = backward_layer(
            incoming, layer_in, params_full, doc_ext, normed, projected, extended, entering
        )
        valid_scale = is_valid.astype(jnp.float32)
        grad_acc = tuple(
            (
                acc_item + valid_scale * grad_item
                for acc_item, grad_item in zip(grad_acc, layer_grads)
            )
        )
        current = lax.dynamic_index_in_dim(grad_buf, batch_idx, 0, keepdims=False)
        grad_buf = lax.dynamic_update_index_in_dim(
            grad_buf, jnp.where(is_valid, grad_input, current), batch_idx, 0
        )
        back_rows = grad_input.astype(jnp.bfloat16)
    owned_sums = lax.psum_scatter(grad_acc, "group", scatter_dimension=0, tiled=True)
    totals = lax.psum(owned_sums, "replica")
    return (out_buf[None], grad_buf[None]) + tuple((total_item[None] for total_item in totals))


def solution(mesh):
    return jax.shard_map(
        on_device,
        mesh=mesh,
        in_specs=(
            P(None, ("group", "replica"), None),
            P(None, ("group", "replica"), None),
            P(None, "group", None),
            P("section", "group"),
            P("section", "group", None),
            P("section", "group", None),
            P("section", "group"),
            P("section", "group"),
            P("section", "group"),
            P("section", "group"),
            P("section", "group"),
            P("section", "group", None),
        ),
        out_specs=(
            P("section", None, ("group", "replica"), None),
            P("section", None, ("group", "replica"), None),
            P("section", "group"),
            P("section", "group", None),
            P("section", "group", None),
            P("section", "group"),
            P("section", "group"),
            P("section", "group"),
            P("section", "group"),
            P("section", "group"),
            P("section", "group", None),
        ),
        check_vma=False,
    )
```

profile of v0, /device:TPU:0, one launch (start us, length us, event | category | flops | bytes accessed | tf_op | source)
XLA Modules:
  0.0 1454.3 jit_solution(10178317865437386804)
XLA Ops:
  18.1 11.9 all-reduce.56
  34.6 11.6 all-gather.1
  51.9 24.5 %all-gather.30.cloned.1.call-done = bf16[1,768,3352]{2,1,0:T(8,128)(2,1)} async-done(((bf16[1,192,3352]{2,1,0:T(8,128)(2,1)}), bf16[1,768,3352]{2,1,0:T(8,128)(2,1)}) %all-gather.30.cloned.1.call-update) | async-done | bytes 5148688 | tf_op jit(solution)/shard_map/all_gather | solution.py:182
  76.4 4.8 fusion.67
  102.1 5.4 divide_multiply_fusion.2
  117.8 8.2 all-gather.8
  132.3 9.1 all-gather.15
  146.2 33.5 %all-gather.32.cloned.1.call-done = f32[96,64,128]{2,1,0:T(8,128)} async-done(((f32[24,64,128]{2,1,0:T(8,128)}), f32[96,64,128]{2,1,0:T(8,128)}) %all-gather.32.cloned.1.call-update) | async-done | bytes 3145744 | tf_op jit(solution)/shard_map/all_gather | solution.py:29
  182.3 9.7 fusion.221
  197.6 20.1 %all-gather.34.cloned.1.call-done = bf16[1,1536,768]{2,1,0:T(8,128)(2,1)} async-done(((bf16[1,384,768]{2,1,0:T(8,128)(2,1)}), bf16[1,1536,768]{2,1,0:T(8,128)(2,1)}) %all-gather.34.cloned.1.call-update) | async-done | bytes 2359312 | tf_op jit(solution)/shard_map/all_gather | solution.py:189
  229.4 4.9 fusion.65
  248.9 5.6 divide_multiply_fusion.1
  277.1 9.1 all-gather.16
  291.1 34.5 %all-gather.36.cloned.1.call-done = f32[96,64,128]{2,1,0:T(8,128)} async-done(((f32[24,64,128]{2,1,0:T(8,128)}), f32[96,64,128]{2,1,0:T(8,128)}) %all-gather.36.cloned.1.call-update) | async-done | bytes 3145744 | tf_op jit(solution)/shard_map/all_gather | solution.py:29
  328.2 9.7 fusion.219
  356.6 4.7 pad_maximum_fusion
  365.3 5.1 copy.830
  388.2 5.4 fusion.190
  408.6 11.4 all-gather.17
  421.4 10.4 fusion.189
  438.1 9.9 fusion.29
  448.1 18.5 %all-gather.38.cloned.1.call-done = f32[96,64,128]{2,1,0:T(8,128)} async-done(((f32[24,64,128]{2,1,0:T(8,128)}), f32[96,64,128]{2,1,0:T(8,128)}) %all-gather.38.cloned.1.call-update) | async-done | bytes 3145744 | tf_op jit(solution)/shard_map/all_gather | solution.py:29
  478.1 4.6 multiply_reduce_fusion.23
  490.7 5.1 copy.858
  500.4 14.8 %all-gather.18 = f32[4,1,24]{2,1,0:T(1,128)} all-gather(f32[1,1,24]{2,1,0:T(1,128)S(1)} %bitcast.1033), channel_id=1, replica_groups=mesh['section'=2,'group'=4,'replica'=4] {'replica'}, dimensions={0}, use_global_device_ids=true | all-gather | bytes 480 | tf_op jit(solution)/shard_map/all_gather | solution.py:29
  530.7 25.2 %all-gather.40.cloned.1.call-done = f32[96,64,128]{2,1,0:T(8,128)} async-done(((f32[24,64,128]{2,1,0:T(8,128)}), f32[96,64,128]{2,1,0:T(8,128)}) %all-gather.40.cloned.1.call-update) | async-done | bytes 3145744 | tf_op jit(solution)/shard_map/all_gather | solution.py:29
  556.0 6.2 while.57
  578.7 10.9 fusion.70
  627.9 4.8 fusion.309
  632.7 6.8 bitcast_add_fusion.10
  642.7 4.6 fusion.599
  650.3 4.9 convolution_bitcast_fusion.2
  673.5 9.5 fusion.17
  693.7 5.1 fusion.342
  716.7 5.1 copy.886
  739.8 11.2 all-gather.19
  753.8 24.7 %all-gather.42.cloned.1.call-done = f32[96,64,128]{2,1,0:T(8,128)} async-done(((f32[24,64,128]{2,1,0:T(8,128)}), f32[96,64,128]{2,1,0:T(8,128)}) %all-gather.42.cloned.1.call-update) | async-done | bytes 3145744 | tf_op jit(solution)/shard_map/all_gather | solution.py:29
  778.6 6.1 while.58
  814.6 10.9 fusion.72
  864.1 4.8 fusion.315
  868.9 6.8 bitcast_add_fusion.8
  878.7 4.5 fusion.598
  886.3 4.9 convolution_bitcast_fusion.1
  909.7 9.5 fusion.5
  929.9 5.0 fusion.346
  952.4 4.6 fusion.351
  958.6 5.7 fusion.401
  972.0 10.7 all-gather.20
  982.7 7.2 fusion.399
  991.3 7.1 multiply_add_fusion.1
  998.5 14.7 %all-gather.44.cloned.1.call-done = f32[96,64,128]{2,1,0:T(8,128)} async-done(((f32[24,64,128]{2,1,0:T(8,128)}), f32[96,64,128]{2,1,0:T(8,128)}) %all-gather.44.cloned.1.call-update) | async-done | bytes 3145744 | tf_op jit(solution)/shard_map/all_gather | solution.py:29
  1013.3 6.5 while.59
  1035.0 12.6 fusion.74
  1056.9 4.6 multiply_reduce_fusion.26
  1096.5 8.2 bitcast_add_fusion.6
  1107.7 4.5 fusion.597
  1129.7 14.7 %multiply_reduce_fusion.17 = (f32[1792]{0:T(1024)}, f32[1792]{0:T(1024)}, f32[1792]{0:T(1024)}, f32[1792]{0:T(1024)}, f32[1792]{0:T(1024)}, /*index=5*/f32[1792]...) fusion(f32[256,1792]{1,0:T(8,128)S(1)} %copy-done.43, ...), kind=kLoop, calls=%fused_computation.265 | loop fusion | flops 20163584 | bytes 31290392 | tf_op jit(solution)/shard_map/transpose(jvp())/reduce_sum | solution.py:85
  1152.5 9.1 multiply_add_fusion
  1177.5 8.8 fusion.217
  1191.0 75.0 %reduce-scatter.6.cloned.1.call-done = f32[192,3352]{1,0:T(8,128)} async-done(((f32[768,3352]{1,0:T(8,128)}), f32[192,3352]{1,0:T(8,128)}) %reduce-scatter.6.cloned.1.call-update) | async-done | bytes 2574352 | tf_op jit(solution)/shard_map/reduce_scatter | solution.py:361
  1278.9 5.8 fusion.350
  1284.7 15.4 %all-reduce.55 = (f32[768]{0:T(1024)S(1)}, f32[1792]{0:T(1024)S(1)}, f32[24]{0:T(128)S(1)}, f32[24]{0:T(128)S(1)}, f32[24]{0:T(128)S(1)}, /*index=5*/f32[1536]{0:T(1024)S(1)}) all-reduce(f32[768]{0:T(1024)S(1)} %multiply_add_fusion.11, ...), channel_id=17, replica_groups=mesh['section'=2,'group'=4,'replica'=4] {'group'}, use_global_device_ids=true, to_apply=%region_105.107.clone | all-reduce | flops 4168 | bytes 33344
  1304.1 20.1 %all-reduce.53 = (f32[1,192]{1,0:T(1,128)}, f32[1,448,4]{1,2,0:T(4,128)}, f32[1,448]{1,0:T(1,128)}, f32[1,6]{1,0:T(1,128)}, f32[1,6]{1,0:T(1,128)}, /*index=5*/f32[1,6]{1,0:T(1,128)}, f32[1,384]{1,0:T(1,128)}) all-reduce(f32[1,192]{1,0:T(1,128)S(1)} %bitcast.1026, ...), channel_id=1, replica_groups=mesh['section'=2,'group'=4,'replica'=4] {'replica'}, use_global_device_ids=true, to_apply=%region_106.108 | all-reduce | flops 2834 | bytes 22672 | tf_op jit(solution)/shard_map/psum | solution.py:362
  1324.2 118.3 %all-reduce.59.cloned.1.call-done = (f32[1,192,3352]{2,1,0:T(8,128)}, f32[1,384,768]{2,1,0:T(8,128)}) async-done(((f32[1,192,3352]{2,1,0:T(8,128)}, f32[1,384,768]{2,1,0:T(8,128)}), (f32[1,192,3352]{2,1,0:T(8,128)}, f32[1,384,768]{2,1,0:T(8,128)})) %all-reduce.59.cloned.1.call-update) | async-done | bytes 3754000 | tf_op jit(solution)/shard_map/psum | solution.py:362
  (1346 shorter events, 618.3 us)
Async XLA Ops:
  7.2 22.9 %copy-start.349 = (s32[2,1,8]{2,1,0:T(1,128)S(1)}, s32[2,1,8]{2,1,0:T(1,128)}, u32[]{:S(2)}) copy-start(s32[2,1,8]{2,1,0:T(1,128)} %param.27) | copy-start | bytes 196
  7.2 27.2 %copy-start.362 = (bf16[1,448,4]{1,2,0:T(4,128)(2,1)S(1)}, bf16[1,448,4]{1,2,0:T(4,128)(2,1)}, u32[]{:S(2)}) copy-start(bf16[1,448,4]{1,2,0:T(4,128)(2,1)} %param.30) | copy-start | bytes 10756
  7.2 69.2 %all-gather.30.cloned.1.call-start = ((), (), s32[]{:S(2)}) async-start(), calls=%async_computation.5 | async-start | bytes 6635520 | tf_op jit(solution)/shard_map/all_gather | solution.py:182
  7.9 171.8 %all-gather.32.cloned.1.call-start = ((), (), s32[]{:S(2)}) async-start(), calls=%async_computation.6 | async-start | bytes 3932160 | tf_op jit(solution)/shard_map/all_gather | solution.py:29
  15.7 33.2 %copy-start.192 = (bf16[256,768]{1,0:T(8,128)(2,1)}, bf16[256,768]{1,0:T(8,128)(2,1)S(1)}, u32[]{:S(2)}) copy-start(bf16[256,768]{1,0:T(8,128)(2,1)S(1)} %broadcast.966) | copy-start | bytes 1179652
  15.7 35.2 %collective-permute-start = (bf16[256,768]{1,0:T(8,128)(2,1)S(1)}, bf16[256,768]{1,0:T(8,128)(2,1)S(1)}, u32[]{:S(2)}, u32[]{:S(2)}) collective-permute-start(bf16[256,768]{1,0:T(8,128)(2,1)S(1)} %broadcast.966), channel_id=1, source_target_pairs={{0,16},{1,17},{2,18},{3,19},{4,20},{5,21},{6,22},{7,23},{8,24},{9,... | collective-permute-start | bytes 1179656 | tf_op jit(solution)/shard_map/ppermute | solution.py:22
  30.0 18.9 %copy-start.388 = (bf16[24]{0:T(256)(128)(2,1)}, bf16[24]{0:T(256)(128)(2,1)S(1)}, u32[]{:S(2)}) copy-start(bf16[24]{0:T(256)(128)(2,1)S(1)} %get-tuple-element.1147) | copy-start | bytes 148
  30.0 46.3 %copy-start.194 = (f32[768]{0:T(1024)}, f32[768]{0:T(1024)S(1)}, u32[]{:S(2)}) copy-start(f32[768]{0:T(1024)S(1)} %convert_element_type.499) | copy-start | bytes 9220
  30.0 64.4 %copy-start.240 = (f32[24]{0:T(128)}, f32[24]{0:T(128)S(1)}, u32[]{:S(2)}) copy-start(f32[24]{0:T(128)S(1)} %convert_element_type.500) | copy-start | bytes 292
  34.4 67.7 %copy-start.210 = (f32[1792]{0:T(1024)}, f32[1792]{0:T(1024)S(1)}, u32[]{:S(2)}) copy-start(f32[1792]{0:T(1024)S(1)} %convert_element_type.498) | copy-start | bytes 21508
  47.2 36.3 %copy-start.297 = (f32[24]{0:T(128)}, f32[24]{0:T(128)S(1)}, u32[]{:S(2)}) copy-start(f32[24]{0:T(128)S(1)} %convert_exponential_fusion) | copy-start | bytes 292
  49.0 53.1 %copy-start.170 = (f32[1792]{0:T(1024)}, f32[1792]{0:T(1024)S(1)}, u32[]{:S(2)}) copy-start(f32[1792]{0:T(1024)S(1)} %get-tuple-element.1063) | copy-start | bytes 21508
  49.0 53.1 %copy-start.176 = (f32[1792]{0:T(1024)}, f32[1792]{0:T(1024)S(1)}, u32[]{:S(2)}) copy-start(f32[1792]{0:T(1024)S(1)} %get-tuple-element.1064) | copy-start | bytes 21508
  49.0 53.1 %copy-start.182 = (f32[1792]{0:T(1024)}, f32[1792]{0:T(1024)S(1)}, u32[]{:S(2)}) copy-start(f32[1792]{0:T(1024)S(1)} %get-tuple-element.1065) | copy-start | bytes 21508
  51.9 29.4 %copy-start.340 = (f32[256]{0:T(256)}, f32[256]{0:T(256)S(1)}, u32[]{:S(2)}) copy-start(f32[256]{0:T(256)S(1)} %add_rsqrt_fusion.5) | copy-start | bytes 3076
  81.2 45.0 %copy-start.8 = (f32[256,3352]{0,1:T(8,128)}, f32[256,3352]{0,1:T(8,128)S(1)}, u32[]{:S(2)}) copy-start(f32[256,3352]{0,1:T(8,128)S(1)} %fusion.67) | copy-start | bytes 10297348
  89.8 12.2 collective-permute-start.1
  116.9 100.7 %all-gather.34.cloned.1.call-start = ((), (), s32[]{:S(2)}) async-start(), calls=%async_computation.7 | async-start | bytes 2949120 | tf_op jit(solution)/shard_map/all_gather | solution.py:189
  117.7 207.9 %all-gather.36.cloned.1.call-start = ((), (), s32[]{:S(2)}) async-start(), calls=%async_computation.8 | async-start | bytes 3932160 | tf_op jit(solution)/shard_map/all_gather | solution.py:29
  126.2 56.1 %copy-start.356 = (f32[24]{0:T(128)}, f32[24]{0:T(128)S(1)}, u32[]{:S(2)}) copy-start(f32[24]{0:T(128)S(1)} %convert_element_type.502) | copy-start | bytes 292
  195.0 22.7 %copy-start.73 = (bf16[256,768]{1,0:T(8,128)(2,1)S(1)}, bf16[256,768]{1,0:T(8,128)(2,1)}, u32[]{:S(2)}) copy-start(bf16[256,768]{1,0:T(8,128)(2,1)} %get-tuple-element.1192) | copy-start | bytes 1179652
  222.8 6.4 collective-permute-start.2
  238.6 9.7 collective-permute-start.3
  262.7 203.9 %all-gather.38.cloned.1.call-start = ((), (), s32[]{:S(2)}) async-start(), calls=%async_computation.9 | async-start | bytes 3932160 | tf_op jit(solution)/shard_map/all_gather | solution.py:29
  347.5 4.8 collective-permute-start.4
  374.2 10.1 collective-permute-start.5
  400.4 20.9 %copy-start.172 = (f32[1792]{0:T(1024)S(1)}, f32[1792]{0:T(1024)}, u32[]{:S(2)}) copy-start(f32[1792]{0:T(1024)} %copy-done.170) | copy-start | bytes 21508
  400.4 20.9 %copy-start.178 = (f32[1792]{0:T(1024)S(1)}, f32[1792]{0:T(1024)}, u32[]{:S(2)}) copy-start(f32[1792]{0:T(1024)} %copy-done.176) | copy-start | bytes 21508
  400.4 20.9 %copy-start.184 = (f32[1792]{0:T(1024)S(1)}, f32[1792]{0:T(1024)}, u32[]{:S(2)}) copy-start(f32[1792]{0:T(1024)} %copy-done.182) | copy-start | bytes 21508
  400.4 20.9 %copy-start.212 = (f32[1792]{0:T(1024)S(1)}, f32[1792]{0:T(1024)}, u32[]{:S(2)}) copy-start(f32[1792]{0:T(1024)} %copy-done.210) | copy-start | bytes 21508
  400.5 155.5 %all-gather.40.cloned.1.call-start = ((), (), s32[]{:S(2)}) async-start(), calls=%async_computation.10 | async-start | bytes 3932160 | tf_op jit(solution)/shard_map/all_gather | solution.py:29
  400.5 5.5 collective-permute-start.6
  404.5 27.3 %copy-start.303 = (f32[256]{0:T(256)}, f32[256]{0:T(256)S(1)}, u32[]{:S(2)}) copy-start(f32[256]{0:T(256)S(1)} %get-tuple-element.1274) | copy-start | bytes 3076
  404.5 27.3 %copy-start.305 = (f32[256]{0:T(256)}, f32[256]{0:T(256)S(1)}, u32[]{:S(2)}) copy-start(f32[256]{0:T(256)S(1)} %get-tuple-element.1275) | copy-start | bytes 3076
  404.5 27.3 %copy-start.307 = (f32[256]{0:T(256)}, f32[256]{0:T(256)S(1)}, u32[]{:S(2)}) copy-start(f32[256]{0:T(256)S(1)} %get-tuple-element.1276) | copy-start | bytes 3076
  405.2 26.6 %copy-start.318 = (f32[256]{0:T(256)}, f32[256]{0:T(256)S(1)}, u32[]{:S(2)}) copy-start(f32[256]{0:T(256)S(1)} %get-tuple-element.1286) | copy-start | bytes 3076
  405.2 26.6 %copy-start.321 = (f32[256]{0:T(256)}, f32[256]{0:T(256)S(1)}, u32[]{:S(2)}) copy-start(f32[256]{0:T(256)S(1)} %get-tuple-element.1287) | copy-start | bytes 3076
  405.2 26.6 %copy-start.324 = (f32[256]{0:T(256)}, f32[256]{0:T(256)S(1)}, u32[]{:S(2)}) copy-start(f32[256]{0:T(256)S(1)} %get-tuple-element.1288) | copy-start | bytes 3076
  405.2 26.6 %copy-start.346 = (f32[256]{0:T(256)}, f32[256]{0:T(256)S(1)}, u32[]{:S(2)}) copy-start(f32[256]{0:T(256)S(1)} %get-tuple-element.1285) | copy-start | bytes 3076
  407.7 24.2 %copy-start.151 = (f32[24,2,128]{2,0,1:T(8,128)}, f32[24,2,128]{2,0,1:T(8,128)S(1)}, u32[]{:S(2)}) copy-start(f32[24,2,128]{2,0,1:T(8,128)S(1)} %reduce-window.238) | copy-start | bytes 73732
  407.9 24.0 %copy-start.312 = (f32[24,2]{0,1:T(2,128)}, f32[24,2]{0,1:T(2,128)S(1)}, u32[]{:S(2)}) copy-start(f32[24,2]{0,1:T(2,128)S(1)} %slice.684) | copy-start | bytes 580
  487.8 290.7 %all-gather.42.cloned.1.call-start = ((), (), s32[]{:S(2)}) async-start(), calls=%async_computation.11 | async-start | bytes 3932160 | tf_op jit(solution)/shard_map/all_gather | solution.py:29
  497.1 18.2 %copy-start.70 = (bf16[256,768]{1,0:T(8,128)(2,1)S(1)}, bf16[256,768]{1,0:T(8,128)(2,1)}, u32[]{:S(2)}) copy-start(bf16[256,768]{1,0:T(8,128)(2,1)} %copy-done.69) | copy-start | bytes 1179652
  497.1 18.2 %copy-start.74 = (bf16[256,768]{1,0:T(8,128)(2,1)S(1)}, bf16[256,768]{1,0:T(8,128)(2,1)}, u32[]{:S(2)}) copy-start(bf16[256,768]{1,0:T(8,128)(2,1)} %get-tuple-element.1192) | copy-start | bytes 1179652
  497.1 18.2 %copy-start.78 = (bf16[256,768]{1,0:T(8,128)(2,1)S(1)}, bf16[256,768]{1,0:T(8,128)(2,1)}, u32[]{:S(2)}) copy-start(bf16[256,768]{1,0:T(8,128)(2,1)} %copy-done.76) | copy-start | bytes 1179652
  500.2 16.9 %copy-start.36 = (f32[256,1792]{1,0:T(8,128)S(1)}, f32[256,1792]{1,0:T(8,128)}, u32[]{:S(2)}) copy-start(f32[256,1792]{1,0:T(8,128)} %get-tuple-element.1179) | copy-start | bytes 5505028
  522.5 48.5 %copy-start.119 = (f32[256,128]{1,0:T(8,128)}, f32[256,128]{1,0:T(8,128)S(1)}, u32[]{:S(2)}) copy-start(f32[256,128]{1,0:T(8,128)S(1)} %get-tuple-element.988) | copy-start | bytes 393220
  522.5 48.5 %copy-start.126 = (f32[256,128]{1,0:T(8,128)}, f32[256,128]{1,0:T(8,128)S(1)}, u32[]{:S(2)}) copy-start(f32[256,128]{1,0:T(8,128)S(1)} %get-tuple-element.986) | copy-start | bytes 393220
  666.6 25.2 %collective-permute-start.7 = (f32[3,1792]{1,0:T(4,128)}, f32[3,1792]{1,0:T(4,128)}, u32[]{:S(2)}, u32[]{:S(2)}) collective-permute-start(f32[3,1792]{1,0:T(4,128)} %pad_add_fusion.5), channel_id=1, source_target_pairs={{1,0},{2,1},{3,2},{5,4},{6,5},{7,6},{9,8},{10,9},{11,10},{13,12},{... | collective-permute-start | bytes 64520 | tf_op jit(solution)/shard_map/ppermute | solution.py:22
  672.6 67.0 %copy-start.226 = (f32[256,24]{0,1:T(8,128)}, f32[256,24]{0,1:T(8,128)S(1)}, u32[]{:S(2)}) copy-start(f32[256,24]{0,1:T(8,128)S(1)} %get-tuple-element.1266) | copy-start | bytes 73732
  698.8 52.2 %copy-start.368 = (f32[256]{0:T(256)}, f32[256]{0:T(256)S(1)}, u32[]{:S(2)}) copy-start(f32[256]{0:T(256)S(1)} %get-tuple-element.1061) | copy-start | bytes 3076
  700.5 3.9 collective-permute-start.8
  714.6 298.6 %all-gather.44.cloned.1.call-start = ((), (), s32[]{:S(2)}) async-start(), calls=%async_computation.12 | async-start | bytes 3932160 | tf_op jit(solution)/shard_map/all_gather | solution.py:29
  902.5 25.6 %collective-permute-start.9 = (f32[3,1792]{1,0:T(4,128)}, f32[3,1792]{1,0:T(4,128)}, u32[]{:S(2)}, u32[]{:S(2)}) collective-permute-start(f32[3,1792]{1,0:T(4,128)} %pad_add_fusion.4), channel_id=1, source_target_pairs={{1,0},{2,1},{3,2},{5,4},{6,5},{7,6},{9,8},{10,9},{11,10},{13,12},{... | collective-permute-start | bytes 64520 | tf_op jit(solution)/shard_map/ppermute | solution.py:22
  935.3 3.9 collective-permute-start.10
  939.2 51.6 %copy-start.88 = (bf16[256,768]{1,0:T(8,128)(2,1)}, bf16[256,768]{1,0:T(8,128)(2,1)S(1)}, u32[]{:S(2)}) copy-start(bf16[256,768]{1,0:T(8,128)(2,1)S(1)} %bitcast_select_fusion.1) | copy-start | bytes 1179652
  949.3 241.7 %reduce-scatter.8.cloned.1.call-start = ((), (), s32[]{:S(2)}) async-start(), calls=%async_computation.4 | async-start | bytes 5898240 | tf_op jit(solution)/shard_map/reduce_scatter | solution.py:361
  998.4 267.5 %reduce-scatter.6.cloned.1.call-start = ((), (), s32[]{:S(2)}) async-start(), calls=%async_computation.3 | async-start | bytes 13271040 | tf_op jit(solution)/shard_map/reduce_scatter | solution.py:361
  1145.9 6.0 collective-permute-start.11
  1161.6 141.3 %reduce-scatter.10.cloned.1.call-start = ((), (), s32[]{:S(2)}) async-start(), calls=%async_computation.13 | async-start | bytes 1146880
  1170.8 17.4 %copy-start.80 = (f32[256,1536]{1,0:T(8,128)}, f32[256,1536]{1,0:T(8,128)S(1)}, u32[]{:S(2)}) copy-start(f32[256,1536]{1,0:T(8,128)S(1)} %copy.924) | copy-start | bytes 4718596
  1190.9 251.6 %all-reduce.59.cloned.1.call-start = ((), (), s32[]{:S(2)}) async-start(), calls=%async_computation.14 | async-start | bytes 7667712 | tf_op jit(solution)/shard_map/psum | solution.py:362
  1278.9 21.7 %copy-start.367 = (f32[256]{0:T(256)S(1)}, f32[256]{0:T(256)}, u32[]{:S(2)}) copy-start(f32[256]{0:T(256)} %get-tuple-element.1060) | copy-start | bytes 3076
  1278.9 21.7 %copy-start.89 = (bf16[256,768]{1,0:T(8,128)(2,1)S(1)}, bf16[256,768]{1,0:T(8,128)(2,1)}, u32[]{:S(2)}) copy-start(bf16[256,768]{1,0:T(8,128)(2,1)} %copy-done.88) | copy-start | bytes 1179652
  (358 other events, 1484.5 us)
Sparse Core Ops, SparseCore 0:
  9.9 66.4 all-gather.29
  117.0 62.6 all-gather.31
  181.5 36.0 all-gather.33
  262.9 62.6 all-gather.35
  400.6 65.9 all-gather.37
  487.9 67.9 all-gather.39
  714.7 63.7 all-gather.41
  949.4 63.7 all-gather.43
  1016.2 55.7 reduce-scatter.7
  1161.8 104.1 reduce-scatter.5
  1268.9 27.0 reduce-scatter.9
  1298.3 144.0 all-reduce.58
where the time goes:
time: 1470 us; the launch traced here: 1450 us
  waiting for transfers between devices  395 us (27%)
  matrix products  330 us (22%)
  local copies, waits for them, and re-layouts  275 us (19%)
  other arithmetic  258 us (18%)
  blocking collectives  134 us (9%)
  between operations  35.8 us (2%)
  starting transfers between devices  25.7 us (2%)
    all_gather x6, waiting for transfers between devices, prefix(): gathered = jax.tree.map(lambda a: lax.all_gather(a, axis), part)  151 us
    psum x1, waiting for transfers between devices, on_device(): totals = lax.psum(owned_sums, 'replica')  118 us
    dot_general x12, matrix products, block_step(): jnp.einsum('hts,shp->thp', weight_mat, inputs, precision=PRECISE)  113 us
    reduce_scatter x2, waiting for transfers between devices, on_device(): lax.psum_scatter(grad_acc, 'group', scatter_dimension=0, tiled=True)  75 us
    all_gather x6, blocking collectives, prefix(): gathered = jax.tree.map(lambda a: lax.all_gather(a, axis), part)  66.4 us
    another operation x48, other arithmetic  52.8 us
    unnamed x822, local copies, waits for them, and re-layouts  49.2 us
    another operation x63, local copies, waits for them, and re-layouts  41.4 us
  transfers between devices with their start and end apart: 24, of which 13 were waited for; matrix products, arithmetic and copies ran while one was open for 31% of the time, Pallas kernels for 0%

commit v1 on v0

v1 whole, which is shorter than its diff:
```python
import jax
import jax.numpy as jnp
from jax import lax
from jax.experimental import pallas as pl
from jax.experimental.pallas import tpu as pltpu
from jax.sharding import PartitionSpec as P

H = 24
P_SIZE = 64
N = 128
KW = 4
INNER = 1536
CONVDIM = 1792
PAIRS = H // 2

EPSILON = 1e-05
PRECISE = lax.Precision.HIGHEST
F32 = jnp.float32
BF16 = jnp.bfloat16


def passed_along(block, axis, distance):
    devices = range(lax.axis_size(axis))
    route = [(i - distance, i) for i in devices if i - distance in devices]
    return lax.ppermute(block, axis, route)


def swapped(block):
    return lax.ppermute(block, "section", [(0, 1), (1, 0)])


def doc_index(lengths_row, first_pos, count_rows):
    position = first_pos + jnp.arange(count_rows, dtype=jnp.int32)
    ends_cum = jnp.cumsum(lengths_row)
    counted = jnp.sum((ends_cum[None, :] <= position[:, None]).astype(jnp.int32), axis=1)
    return jnp.where(position < 0, -1, counted)


def dot_nn(a, b):
    return jnp.dot(a.astype(BF16), b.astype(BF16), preferred_element_type=F32)


def dot_nt(a, b):
    return lax.dot_general(
        a.astype(BF16), b.astype(BF16), (((1,), (1,)), ((), ())), preferred_element_type=F32
    )


def dot_tn(a, b):
    return lax.dot_general(
        a.astype(BF16), b.astype(BF16), (((0,), (0,)), ((), ())), preferred_element_type=F32
    )


def allowed_pairs(doc_col, doc_row):
    length = doc_col.shape[0]
    later = lax.broadcasted_iota(jnp.int32, (length, length), 0)
    earlier = lax.broadcasted_iota(jnp.int32, (length, length), 1)
    return (doc_col == doc_row) & (later >= earlier)


def head_decay(cum_ref, cum_t_ref, head):
    cum = cum_ref[...]
    lane = lax.broadcasted_iota(jnp.int32, cum.shape, 1)
    column = jnp.sum(jnp.where(lane == head, cum, 0.0), axis=1, keepdims=True)
    return jnp.exp(jnp.minimum(column - cum_t_ref[pl.ds(head, 1), :], 0.0))


def intra_fwd_kernel(
    x_ref, b_ref, c_ref, cum_ref, cum_t_ref, step_t_ref, dcol_ref, drow_ref, y_ref, cb_ref
):
    pair = pl.program_id(0)

    @pl.when(pair == 0)
    def _():
        allowed = allowed_pairs(dcol_ref[...], drow_ref[...])
        cb_ref[...] = jnp.where(allowed, dot_nt(c_ref[...], b_ref[...]), 0.0)

    parts = []
    for j in range(2):
        head = 2 * pair + j
        decay = head_decay(cum_ref, cum_t_ref, head)
        weights = decay * cb_ref[...] * step_t_ref[pl.ds(head, 1), :]
        parts.append(dot_nn(weights, x_ref[:, j * P_SIZE : (j + 1) * P_SIZE]))
    y_ref[...] = jnp.concatenate(parts, axis=1)


def whole(shape):
    return pl.BlockSpec(shape, lambda i: (0,) * len(shape))


def per_pair(length):
    return pl.BlockSpec((length, 2 * P_SIZE), lambda i: (0, i))


def intra_forward(inputs, in_basis, out_basis, cum, cum_t, step_t, doc_col, doc_row):
    length = inputs.shape[0]
    return pl.pallas_call(
        intra_fwd_kernel,
        grid=(PAIRS,),
        in_specs=[
            per_pair(length),
            whole((length, N)),
            whole((length, N)),
            whole((length, H)),
            whole((H, length)),
            whole((H, length)),
            whole((length, 1)),
            whole((1, length)),
        ],
        out_specs=per_pair(length),
        out_shape=jax.ShapeDtypeStruct((length, INNER), F32),
        scratch_shapes=[pltpu.VMEM((length, length), F32)],
        compiler_params=pltpu.CompilerParams(vmem_limit_bytes=24 << 20),
        cost_estimate=pl.CostEstimate(
            flops=2 * length * length * INNER, bytes_accessed=8 * length * INNER, transcendentals=H * length * length
        ),
    )(inputs, in_basis, out_basis, cum, cum_t, step_t, doc_col, doc_row)


def intra_bwd_kernel(
    x_ref, dy_ref, b_ref, c_ref, cum_ref, cum_t_ref, step_t_ref, dcol_ref, drow_ref,
    dx_ref, rows_ref, cols_ref, db_ref, dc_ref, cb_ref, acc_ref,
):
    pair = pl.program_id(0)

    @pl.when(pair == 0)
    def _():
        allowed = allowed_pairs(dcol_ref[...], drow_ref[...])
        cb_ref[...] = jnp.where(allowed, dot_nt(c_ref[...], b_ref[...]), 0.0)
        acc_ref[...] = jnp.zeros_like(acc_ref)
        rows_ref[...] = jnp.zeros_like(rows_ref)

    parts = []
    for j in range(2):
        head = 2 * pair + j
        span = slice(j * P_SIZE, (j + 1) * P_SIZE)
        step_row = step_t_ref[pl.ds(head, 1), :]
        decay = head_decay(cum_ref, cum_t_ref, head)
        grad_y = dy_ref[:, span]
        cross = dot_nt(grad_y, x_ref[:, span])
        basis = cb_ref[...]
        scaled = decay * step_row
        acc_ref[...] += scaled * cross
        parts.append(dot_tn(scaled * basis, grad_y))
        product = decay * basis * cross
        cols_ref[pl.ds(head, 1), :] = jnp.sum(product, axis=0, keepdims=True)
        row_sum = jnp.sum(product * step_row, axis=1, keepdims=True)
        lane = lax.broadcasted_iota(jnp.int32, rows_ref.shape, 1)
        rows_ref[...] += jnp.where(lane == head, row_sum, 0.0)
    dx_ref[...] = jnp.concatenate(parts, axis=1)

    @pl.when(pair == PAIRS - 1)
    def _():
        allowed = allowed_pairs(dcol_ref[...], drow_ref[...])
        grad_cb = jnp.where(allowed, acc_ref[...], 0.0)
        dc_ref[...] = dot_nn(grad_cb, b_ref[...])
        db_ref[...] = dot_tn(grad_cb, c_ref[...])


def intra_backward(inputs, grad_y, in_basis, out_basis, cum, cum_t, step_t, doc_col, doc_row):
    length = inputs.shape[0]
    return pl.pallas_call(
        intra_bwd_kernel,
        grid=(PAIRS,),
        in_specs=[
            per_pair(length),
            per_pair(length),
            whole((length, N)),
            whole((length, N)),
            whole((length, H)),
            whole((H, length)),
            whole((H, length)),
            whole((length, 1)),
            whole((1, length)),
        ],
        out_specs=[
            per_pair(length),
            whole((length, H)),
            whole((H, length)),
            whole((length, N)),
            whole((length, N)),
        ],
        out_shape=[
            jax.ShapeDtypeStruct((length, INNER), F32),
            jax.ShapeDtypeStruct((length, H), F32),
            jax.ShapeDtypeStruct((H, length), F32),
            jax.ShapeDtypeStruct((length, N), F32),
            jax.ShapeDtypeStruct((length, N), F32),
        ],
        scratch_shapes=[pltpu.VMEM((length, length), F32), pltpu.VMEM((length, length), F32)],
        compiler_params=pltpu.CompilerParams(vmem_limit_bytes=24 << 20),
        cost_estimate=pl.CostEstimate(
            flops=4 * length * length * INNER, bytes_accessed=12 * length * INNER, transcendentals=H * length * length
        ),
    )(inputs, grad_y, in_basis, out_basis, cum, cum_t, step_t, doc_col, doc_row)


def head_map():
    return (jnp.arange(INNER)[None, :] // P_SIZE == jnp.arange(H)[:, None]).astype(F32)


def expand(per_head):
    return jnp.dot(per_head, head_map(), precision=PRECISE)


def head_sum(values):
    return lax.dot_general(
        values, head_map(), (((1,), (1,)), ((), ())), precision=lax.Precision.HIGH
    )


def combine_states(state, passes, reverse):
    count = lax.axis_size("replica")
    place = lax.axis_index("replica")
    gathered = lax.all_gather(state.astype(BF16), "replica")
    factor = jnp.ones((H,), F32)
    weights = [None] * count
    for source in range(count) if reverse else range(count - 1, -1, -1):
        active = (source > place) if reverse else (source < place)
        weights[source] = jnp.where(active, factor, 0.0)
        factor = jnp.where(active, factor * passes[source], factor)
    total = jnp.zeros((H, P_SIZE, N), F32)
    for source in range(count):
        total = total + weights[source][:, None, None] * gathered[source].astype(F32).reshape(
            H, P_SIZE, N
        )
    return total.reshape(INNER, N)


def rms_factor(values):
    return lax.rsqrt(jnp.mean(values * values, axis=-1, keepdims=True) + EPSILON)


def rms_backward(values, factor, gain, grad):
    scaled = grad * gain[None, :]
    grad_gain = jnp.sum(grad * values * factor, axis=0)
    inner = jnp.mean(scaled * values, axis=-1, keepdims=True)
    return factor * scaled - values * (factor * factor * factor * inner), grad_gain


def silu_slope(values):
    gate = jax.nn.sigmoid(values)
    return gate * (1.0 + values * (1.0 - gate))


def forward_layer(layer_in, params, doc_ext):
    gain_in, w_in, taps, shift, dt_shift, log_rate, skip, gain_out, w_out = params
    length = layer_in.shape[0]
    doc_rows = doc_ext[KW - 1 :]
    before = doc_ext[KW - 2]
    values = layer_in.astype(F32)
    normed = (values * rms_factor(values) * gain_in[None, :]).astype(BF16)
    gate_raw = dot_nn(normed, w_in[:, :INNER])
    rest = dot_nn(normed, w_in[:, INNER:])
    conv_raw = rest[:, :CONVDIM]
    dt_raw = rest[:, CONVDIM:]
    rim = passed_along(conv_raw[length - (KW - 1) :], "replica", 1)
    extended = jnp.concatenate([rim, conv_raw], axis=0)
    conv = shift[None, :]
    for k in range(KW):
        same = (doc_ext[k : k + length] == doc_rows).astype(F32)
        conv = conv + taps[:, k][None, :] * extended[k : k + length] * same[:, None]
    act = jax.nn.silu(conv)
    inputs = act[:, :INNER]
    in_basis = act[:, INNER : INNER + N]
    out_basis = act[:, INNER + N :]
    step = jax.nn.softplus(dt_raw + dt_shift[None, :])
    log_decay = -step * jnp.exp(log_rate)[None, :]
    order = jnp.arange(length)
    lower = (order[:, None] >= order[None, :]).astype(F32)
    cum = jnp.dot(lower, log_decay, precision=PRECISE)
    last = cum[-1]
    inflow = (doc_rows == before).astype(F32)
    weight_in = jnp.exp(cum) * inflow[:, None]
    tail = jnp.exp(last[None, :] - cum) * (doc_rows == doc_rows[-1]).astype(F32)[:, None]
    pass_on = jnp.exp(last) * (doc_rows[-1] == before).astype(F32)
    passes = lax.all_gather(pass_on, "replica")
    tail_wide = expand(tail * step)
    state = dot_tn(tail_wide * inputs, in_basis)
    entering = combine_states(state, passes, False)
    kernel_side = (cum, cum.T, step.T, doc_rows[:, None], doc_rows[None, :])
    intra = intra_forward(inputs, in_basis, out_basis, *kernel_side)
    weight_wide = expand(weight_in)
    inter = weight_wide * dot_nt(out_basis, entering)
    skip_wide = jnp.repeat(skip, P_SIZE)
    mixed = intra + skip_wide[None, :] * inputs + inter
    gated = mixed * jax.nn.silu(gate_raw)
    factor = rms_factor(gated)
    result = (gated * factor * gain_out[None, :]).astype(BF16)
    output = (values + dot_nn(result, w_out)).astype(BF16)
    kept = (
        layer_in, normed, gate_raw, dt_raw, extended, conv, act, step, log_decay, tail, pass_on,
        passes, tail_wide, entering, kernel_side, weight_wide, inter, mixed, factor, result,
    )
    return output, kept


def backward_layer(incoming, kept, params, doc_ext, pending):
    gain_in, w_in, taps, shift, dt_shift, log_rate, skip, gain_out, w_out = params
    (
        layer_in, normed, gate_raw, dt_raw, extended, conv, act, step, log_decay, tail, pass_on,
        passes, tail_wide, entering, kernel_side, weight_wide, inter, mixed, factor, result,
    ) = kept
    length = layer_in.shape[0]
    doc_rows = doc_ext[KW - 1 :]
    inputs = act[:, :INNER]
    in_basis = act[:, INNER : INNER + N]
    out_basis = act[:, INNER + N :]
    grad_result = dot_nt(incoming, w_out)
    silu_gate = jax.nn.silu(gate_raw)
    grad_gated, grad_gain_out = rms_backward(mixed * silu_gate, factor, gain_out, grad_result)
    grad_mixed = grad_gated * silu_gate
    weighted = weight_wide * grad_mixed
    grad_entering = dot_tn(weighted, out_basis)
    carried = combine_states(grad_entering, passes, True)
    grad_inputs, row_sums, col_sums, grad_in_basis, grad_out_basis = intra_backward(
        inputs, grad_mixed, in_basis, out_basis, *kernel_side
    )
    grad_out_weight = dot_tn(result, incoming)
    grad_gate = grad_gated * mixed * silu_slope(gate_raw)
    skip_wide = jnp.repeat(skip, P_SIZE)
    grad_skip = jnp.sum(jnp.sum(grad_mixed * inputs, axis=0).reshape(H, P_SIZE), axis=1)
    grad_inflow = head_sum(grad_mixed * inter)
    grad_out_basis = grad_out_basis + dot_nn(weighted, entering)
    grad_pass = jnp.sum((carried * entering).reshape(H, P_SIZE * N), axis=1)
    back_state = dot_nt(in_basis, carried)
    grad_inputs = grad_inputs + skip_wide[None, :] * grad_mixed + tail_wide * back_state
    grad_in_basis = grad_in_basis + dot_nn(tail_wide * inputs, carried)
    grad_tail = head_sum(inputs * back_state)
    by_tail = grad_tail * tail * step
    by_step = col_sums.T
    grad_step = by_step + grad_tail * tail
    grad_cum = row_sums - by_step * step + grad_inflow - by_tail
    grad_last = jnp.sum(by_tail, axis=0) + grad_pass * pass_on
    order = jnp.arange(length)
    upper = (order[:, None] <= order[None, :]).astype(F32)
    grad_log = jnp.dot(upper, grad_cum, precision=PRECISE) + grad_last[None, :]
    grad_step = grad_step - jnp.exp(log_rate)[None, :] * grad_log
    grad_rate = jnp.sum(grad_log * log_decay, axis=0)
    grad_dt = grad_step * jax.nn.sigmoid(dt_raw + dt_shift[None, :])
    grad_bias = jnp.sum(grad_dt, axis=0)
    grad_act = jnp.concatenate([grad_inputs, grad_in_basis, grad_out_basis], axis=1)
    grad_conv = grad_act * silu_slope(conv)
    grad_shift = jnp.sum(grad_conv, axis=0)
    grad_taps = []
    grad_ext = jnp.zeros((length + KW - 1, CONVDIM), F32)
    for k in range(KW):
        same = (doc_ext[k : k + length] == doc_rows).astype(F32)[:, None] * grad_conv
        grad_taps.append(jnp.sum(same * extended[k : k + length], axis=0))
        grad_ext = grad_ext + jnp.pad(
            taps[:, k][None, :] * same, ((k, KW - 1 - k), (0, 0))
        )
    rim_back = passed_along(grad_ext[: KW - 1], "replica", -1)
    grad_raw = grad_ext[KW - 1 :] + jnp.pad(rim_back, ((length - (KW - 1), 0), (0, 0)))
    grad_proj = jnp.concatenate([grad_gate, grad_raw, grad_dt], axis=1).astype(BF16)
    grad_normed = dot_nt(grad_proj, w_in)
    if pending is not None:
        grad_proj, pending = lax.optimization_barrier((grad_proj, pending))
    grad_in_weight = dot_tn(normed, grad_proj)
    values = layer_in.astype(F32)
    grad_values, grad_gain_in = rms_backward(values, rms_factor(values), gain_in, grad_normed)
    grad_input = incoming.astype(F32) + grad_values
    small = (
        grad_gain_in, jnp.stack(grad_taps, axis=1), grad_shift, grad_bias, grad_rate, grad_skip,
        grad_gain_out,
    )
    return grad_input, grad_in_weight, grad_out_weight, small, pending


def packed_halves(w_in, w_out, groups):
    rows = w_in.shape[0] // groups // 2
    pairs = w_out.reshape(groups, 2, 2, rows, w_out.shape[1])
    return jnp.concatenate(
        [pairs[:, :, 0], pairs[:, :, 1], w_in.reshape(groups, 2, rows, w_in.shape[1])], axis=-1
    )


def unpacked(first, second, width):
    full = jnp.stack([first, second], axis=1)
    groups, _, rows, _ = full.shape
    w_in = full[..., 2 * width :].reshape(groups * 2 * rows, -1)
    w_out = jnp.stack([full[..., :width], full[..., width : 2 * width]], axis=2)
    return w_in, w_out.reshape(groups * 4 * rows, width)


def reduce_layer(grad_in, grad_out, section_idx):
    groups = lax.axis_size("group")
    halves = packed_halves(grad_in.astype(BF16), grad_out.astype(BF16), groups)
    away = lax.dynamic_index_in_dim(halves, 1 - section_idx, 1, keepdims=False)
    here = lax.dynamic_index_in_dim(halves, section_idx, 1, keepdims=False)
    both = (here.astype(F32) + swapped(away).astype(F32)).astype(BF16)
    owned = lax.psum_scatter(both, "group", scatter_dimension=0, tiled=False)
    return lax.psum(owned, "replica")


def on_device(
    tokens, out_grad, doc_lengths, norm_gain, in_weight, conv_weight, conv_bias, dt_bias, a_log,
    skip_gain, out_norm_gain, out_weight,
):
    row_count = tokens.shape[1]
    section_idx = lax.axis_index("section")
    at_first = section_idx == 0
    groups = lax.axis_size("group")
    first_pos = lax.axis_index("replica") * row_count - (KW - 1)
    smalls = (norm_gain, conv_weight, conv_bias, dt_bias, a_log, skip_gain, out_norm_gain)

    width = tokens.shape[2]

    own_halves = packed_halves(in_weight[0], out_weight[0], 1)[0]
    keep = lax.dynamic_index_in_dim(own_halves, section_idx, 0, keepdims=False)
    got = swapped(lax.dynamic_index_in_dim(own_halves, 1 - section_idx, 0, keepdims=False))
    half_first = jnp.where(at_first, keep, got)
    half_second = jnp.where(at_first, got, keep)

    packed = jnp.concatenate([item.reshape(-1) for item in smalls])
    small_own = lax.all_gather(packed, "group")
    small_got = swapped(small_own)
    small_all = jnp.stack(
        [jnp.where(at_first, small_own, small_got), jnp.where(at_first, small_got, small_own)]
    )

    gathered_first = lax.all_gather(half_first, "group")
    gathered_first, half_second = lax.optimization_barrier((gathered_first, half_second))
    weights = []
    for mine in (gathered_first, lax.all_gather(half_second, "group")):
        other = swapped(mine)
        weights.append(
            unpacked(jnp.where(at_first, mine, other), jnp.where(at_first, other, mine), width)
        )
    w_in = (weights[0][0], weights[1][0])
    w_out = (weights[0][1], weights[1][1])
    layer_params = []
    for layer in range(2):
        pieces = []
        start = 0
        for item in smalls:
            size = item.size
            piece = small_all[layer, :, start : start + size].astype(F32)
            pieces.append(piece.reshape((groups * item.shape[1],) + item.shape[2:]))
            start += size
        layer_params.append(
            (pieces[0], w_in[layer]) + tuple(pieces[1:]) + (w_out[layer],)
        )

    lengths_row = lax.dynamic_index_in_dim(doc_lengths[:, 0, :], section_idx, 0, keepdims=False)
    doc_ext = doc_index(lengths_row, first_pos, row_count + KW - 1)
    own_tokens = lax.dynamic_index_in_dim(tokens, section_idx, 0, keepdims=False)
    own_grad = lax.dynamic_index_in_dim(out_grad, section_idx, 0, keepdims=False)

    hidden, kept_first = forward_layer(own_tokens, layer_params[0], doc_ext)
    final, kept_second = forward_layer(hidden, layer_params[1], doc_ext)
    grad_hidden, gin_second, gout_second, small_second, _ = backward_layer(
        own_grad, kept_second, layer_params[1], doc_ext, None
    )
    reduced_second = reduce_layer(gin_second, gout_second, section_idx)
    grad_tokens, gin_first, gout_first, small_first, reduced_second = backward_layer(
        grad_hidden.astype(BF16), kept_first, layer_params[0], doc_ext, reduced_second
    )
    reduced_first = reduce_layer(gin_first, gout_first, section_idx)

    mine = jnp.where(at_first, reduced_first, reduced_second)
    theirs = swapped(jnp.where(at_first, reduced_second, reduced_first))
    grad_in_weight, grad_out_weight = unpacked(
        jnp.where(at_first, mine, theirs)[None], jnp.where(at_first, theirs, mine)[None], width
    )
    grad_in_weight = grad_in_weight.astype(F32)
    grad_out_weight = grad_out_weight.astype(F32)

    def by_batch(first, second):
        mine = jnp.where(at_first, first, second)
        got = swapped(jnp.where(at_first, second, first))
        return jnp.stack([jnp.where(at_first, mine, got), jnp.where(at_first, got, mine)])

    outs = by_batch(hidden, final)
    in_grads = by_batch(grad_tokens, grad_hidden)

    flat_first, flat_second = (
        jnp.concatenate([item.reshape(groups, -1) for item in small], axis=1)
        for small in (small_first, small_second)
    )
    flat = jnp.where(at_first, flat_first, flat_second)
    flat = flat + swapped(jnp.where(at_first, flat_second, flat_first))
    flat = lax.psum_scatter(flat, "group", scatter_dimension=0, tiled=False)
    flat = lax.psum(flat, "replica")
    small_out = []
    start = 0
    for item in smalls:
        small_out.append(flat[start : start + item.size].reshape(item.shape))
        start += item.size
    return (
        outs[None],
        in_grads[None],
        small_out[0],
        grad_in_weight[None],
        small_out[1],
        small_out[2],
        small_out[3],
        small_out[4],
        small_out[5],
        small_out[6],
        grad_out_weight[None],
    )


def solution(mesh):
    return jax.shard_map(
        on_device,
        mesh=mesh,
        in_specs=(
            P(None, ("group", "replica"), None),
            P(None, ("group", "replica"), None),
            P(None, "group", None),
            P("section", "group"),
            P("section", "group", None),
            P("section", "group", None),
            P("section", "group"),
            P("section", "group"),
            P("section", "group"),
            P("section", "group"),
            P("section", "group"),
            P("section", "group", None),
        ),
        out_specs=(
            P("section", None, ("group", "replica"), None),
            P("section", None, ("group", "replica"), None),
            P("section", "group"),
            P("section", "group", None),
            P("section", "group", None),
            P("section", "group"),
            P("section", "group"),
            P("section", "group"),
            P("section", "group"),
            P("section", "group"),
            P("section", "group", None),
        ),
        check_vma=False,
    )
```

time: 1470 us -> 715 us (0.49)
  matrix products: 330 us -> 80.5 us
  local copies, waits for them, and re-layouts: 275 us -> 118 us
  other arithmetic: 258 us -> 108 us
  waiting for transfers between devices: 395 us -> 264 us
  blocking collectives: 134 us -> 66.4 us
  Pallas kernels: 0 us -> 35.2 us
  between operations: 35.8 us -> 19.1 us
    dot_general x78 -> x38, matrix products: 330 us -> 80.5 us  [the longest x8 23 us: dot_nt(): lax.dot_general(a.astype(BF16), b.astype(BF16), (((1,), (1,)), ((), ())),...]
    all_gather x8 -> x6, waiting for transfers between devices: 196 us -> 96.1 us  [the longest x1 52.4 us: on_device(): gathered_first = lax.all_gather(half_first, 'group')]
    reduce_scatter x2 -> x0, waiting for transfers between devices: 75 us -> none  [on_device(): lax.psum_scatter(grad_acc, 'group', scatter_dimension=0, tiled=True)]
    all_gather x8 -> x2, blocking collectives: 86.2 us -> 18 us  [forward_layer(): passes = lax.all_gather(pass_on, 'replica')]
    unnamed x13 -> x12, waiting for transfers between devices: 1.53 us -> 60.2 us
    mul x36 -> x8, other arithmetic: 68.3 us -> 9.93 us  [the longest x2 8.63 us: forward_layer(): act = jax.nn.silu(conv)]
    another operation x60 -> x19, other arithmetic: 66.9 us -> 18.2 us  [the longest x6 9.03 us: unpacked(): full = jnp.stack([first, second], axis=1)]
    mul x38 -> x26, local copies, waits for them, and re-layouts: 51 us -> 4.26 us  [the longest x24 3.51 us: combine_states(): weights[source][:, None, None]]
  transfers between devices with their start and end apart: 24 -> 24, of which waited for: 13 -> 13; matrix products, arithmetic and copies ran while one was open for 31% -> 23% of each run, Pallas kernels for 0% -> 5%
where the time goes in v1:
time: 715 us; the launch traced here: 705 us
  waiting for transfers between devices  264 us (37%)
  local copies, waits for them, and re-layouts  118 us (17%)
  other arithmetic  108 us (15%)
  matrix products  80.5 us (11%)
  blocking collectives  66.4 us (9%)
  Pallas kernels  35.2 us (5%)
  between operations  19.1 us (3%)
  starting transfers between devices  12.8 us (2%)
    psum x2, waiting for transfers between devices, reduce_layer(): return lax.psum(owned, 'replica')  97.5 us
    unnamed x12, waiting for transfers between devices  60.2 us
    unnamed x447, local copies, waits for them, and re-layouts  52.9 us
    all_gather x1, waiting for transfers between devices, on_device(): gathered_first = lax.all_gather(half_first, 'group')  52.4 us
    all_gather x4, waiting for transfers between devices, combine_states(): gathered = lax.all_gather(state.astype(BF16), 'replica')  41.3 us
    unnamed x2, blocking collectives  32 us
    pallas_call x2, Pallas kernels, intra_backward(): pl.pallas_call(intra_bwd_kernel, grid=(PAIRS,), in_specs=[per_pair(length...  23.6 us
    dot_general x8, matrix products, dot_nt(): lax.dot_general(a.astype(BF16), b.astype(BF16), (((1,), (1,)), ((), ())),...  23 us
  transfers between devices with their start and end apart: 24, of which 13 were waited for; matrix products, arithmetic and copies ran while one was open for 23% of the time, Pallas kernels for 5%

profile of v1, /device:TPU:0, one launch (start us, length us, event | category | flops | bytes accessed | tf_op | source)
XLA Modules:
  0.0 705.0 jit_solution(14267143300758013642)
XLA Ops:
  11.3 2.4 collective-permute-done.1
  13.8 2.7 bitcast_select_fusion
  16.5 52.4 %all-gather.16.cloned.1.call-done = bf16[384,4888]{1,0:T(8,128)(2,1)} async-done(((bf16[96,4888]{1,0:T(8,128)(2,1)}), bf16[384,4888]{1,0:T(8,128)(2,1)}) %all-gather.16.cloned.1.call-update) | async-done | bytes 3754000 | tf_op jit(solution)/shard_map/all_gather | solution.py:423
  71.1 15.3 %all-reduce.10 = bf16[11336]{0:T(1024)(128)(2,1)S(1)} all-reduce(bf16[11336]{0:T(1024)(128)(2,1)S(1)} %dynamic-update-slice), channel_id=2, replica_groups=mesh['section'=2,'group'=4,'replica'=4] {'group'}, use_global_device_ids=true, to_apply=%add.10 | all-reduce | flops 11336 | bytes 45344
  95.4 3.7 select_bitcast_fusion.3
  106.3 3.3 collective-permute-start.3
  110.1 2.1 fusion.139
  115.4 2.6 fusion.19
  130.3 9.0 %all-gather.7 = f32[4,1,24]{2,1,0:T(1,128)S(1)} all-gather(f32[1,1,24]{2,1,0:T(1,128)S(1)} %bitcast.403), channel_id=1, replica_groups=mesh['section'=2,'group'=4,'replica'=4] {'replica'}, dimensions={0}, use_global_device_ids=true | all-gather | bytes 480 | tf_op jit(solution)/shard_map/all_gather | solution.py:278
  139.3 2.3 all-gather.20.cloned.1.call-done
  146.0 3.7 fusion.10
  150.6 5.8 shard_map.203
  157.8 23.1 %all-gather.18.cloned.1.call-done = bf16[6144,128]{1,0:T(8,128)(2,1)} async-done(((bf16[1536,128]{1,0:T(8,128)(2,1)}), bf16[6144,128]{1,0:T(8,128)(2,1)}) %all-gather.18.cloned.1.call-update) | async-done | bytes 1572880 | tf_op jit(solution)/shard_map/all_gather | solution.py:216
  180.9 2.4 fusion.66
  191.8 2.5 select_bitcast_fusion.1
  203.3 2.6 collective-permute-start.5
  205.9 2.8 fusion.137
  208.7 2.9 slice.524
  211.6 2.8 copy.226
  214.5 6.0 fusion.18
  228.6 9.0 %all-gather.8 = f32[4,1,24]{2,1,0:T(1,128)S(1)} all-gather(f32[1,1,24]{2,1,0:T(1,128)S(1)} %bitcast.404), channel_id=1, replica_groups=mesh['section'=2,'group'=4,'replica'=4] {'replica'}, dimensions={0}, use_global_device_ids=true | all-gather | bytes 480 | tf_op jit(solution)/shard_map/all_gather | solution.py:278
  240.1 2.7 fusion.138
  242.7 3.9 fusion.8
  247.6 5.8 shard_map.204
  255.9 3.6 all-gather.22.cloned.1.call-done
  259.5 2.4 fusion.78
  269.6 2.7 multiply_reduce_fusion.9
  281.6 11.8 %shard_map.205 = (f32[256,1536]{1,0:T(8,128)S(1)}, f32[256,24]{1,0:T(8,128)S(1)}, f32[24,256]{1,0:T(8,128)S(1)}, f32[256,128]{1,0:T(8,128)S(1)}, f32[256,128]{1,0:T(8,128)S(1)}) custom-call(f32[256,1536]{1,0:T(8,128)S(1)} %copy-done.3, f32[256,1536]{1,0:T(8,128)S(1)} %get-tuple-element.119.dy_ref, f32[256,128]{1,0:T(8,128)S(1)} %copy-done.19, ...), custom_call_target="tpu_custom_call" | custom-call | flops 402653184 | bytes 4718592 | tf_op jit(solution)/shard_map/pallas_call | solution.py:163
  298.1 2.3 fusion.230
  300.4 2.4 convolution_convert_fusion.2
  304.4 6.4 all-gather.24.cloned.1.call-done
  310.9 2.4 fusion.88
  313.4 2.1 multiply_add_fusion.3
  316.3 2.6 multiply_reduce_fusion.3
  326.1 4.6 fusion.74
  343.6 5.1 convolution_convert_fusion.1
  348.7 7.9 %copy.213 = bf16[768,3352]{1,0:T(8,128)(2,1)} copy(bf16[768,3352]{0,1:T(8,128)(2,1)} %convolution_convert_fusion.1) | data formatting | bytes 10297344 | tf_op jit(solution)/shard_map/convert_element_type | solution.py:389
  356.6 3.6 pad_maximum_fusion
  360.3 2.2 dynamic-slice_bitcast_fusion.1
  362.5 2.1 copy-done.41
  364.6 5.1 fusion.108
  373.8 2.8 multiply_reduce_fusion.11
  379.0 6.0 fusion.1
  387.8 11.8 %shard_map.206 = (f32[256,1536]{1,0:T(8,128)S(1)}, f32[256,24]{1,0:T(8,128)S(1)}, f32[24,256]{1,0:T(8,128)S(1)}, f32[256,128]{1,0:T(8,128)S(1)}, f32[256,128]{1,0:T(8,128)S(1)}) custom-call(f32[256,1536]{1,0:T(8,128)S(1)} %get-tuple-element.179.x_ref, f32[256,1536]{1,0:T(8,128)S(1)} %get-tuple-element.114.dy_ref, f32[256,128]{1,0:T(8,128)S(1)} %copy-done.15, ...), custom_call_target="tpu_custom_call" | custom-call | flops 402653184 | bytes 4718592 | tf_op jit(solution)/shard_map/pallas_call | solution.py:163
  406.1 2.1 convolution_convert_fusion.3
  409.7 8.2 %all-gather.26.cloned.1.call-done = bf16[6144,128]{1,0:T(8,128)(2,1)} async-done(((bf16[1536,128]{1,0:T(8,128)(2,1)}), bf16[6144,128]{1,0:T(8,128)(2,1)}) %all-gather.26.cloned.1.call-update) | async-done | bytes 1572880 | tf_op jit(solution)/shard_map/all_gather | solution.py:216
  417.9 2.3 fusion.98
  420.3 3.3 multiply_add_fusion.2
  425.2 4.2 fusion.62
  430.2 5.7 multiply_reduce_fusion.7
  442.4 27.2 %reduce-scatter.7.cloned.1.call-done = bf16[1,96,4888]{2,1,0:T(8,128)(2,1)} async-done(((bf16[4,96,4888]{2,1,0:T(8,128)(2,1)}), bf16[1,96,4888]{2,1,0:T(8,128)(2,1)}) %reduce-scatter.7.cloned.1.call-update) | async-done | bytes 938512
  472.6 48.9 %all-reduce.17.cloned.1.call-done = bf16[96,4888]{1,0:T(8,128)(2,1)} async-done(((bf16[96,4888]{1,0:T(8,128)(2,1)}), bf16[96,4888]{1,0:T(8,128)(2,1)}) %all-reduce.17.cloned.1.call-update) | async-done | bytes 938512 | tf_op jit(solution)/shard_map/psum | solution.py:394
  521.5 4.9 convolution_convert_fusion
  526.3 8.0 %copy.214 = bf16[768,3352]{1,0:T(8,128)(2,1)} copy(bf16[768,3352]{0,1:T(8,128)(2,1)} %convolution_convert_fusion) | data formatting | bytes 10297344 | tf_op jit(solution)/shard_map/convert_element_type | solution.py:389
  534.3 3.4 pad_maximum_fusion.1
  538.1 6.6 collective-permute-done.12
  544.7 2.8 fusion
  549.0 3.3 broadcast_select_fusion.2
  558.4 5.5 fusion.116
  563.9 32.9 %reduce-scatter.9.cloned.1.call-done = bf16[1,96,4888]{2,1,0:T(8,128)(2,1)} async-done(((bf16[4,96,4888]{2,1,0:T(8,128)(2,1)}), bf16[1,96,4888]{2,1,0:T(8,128)(2,1)}) %reduce-scatter.9.cloned.1.call-update) | async-done | bytes 938512
  596.8 2.4 fusion.123
  600.1 48.6 %all-reduce.19.cloned.1.call-done = bf16[96,4888]{1,0:T(8,128)(2,1)} async-done(((bf16[96,4888]{1,0:T(8,128)(2,1)}), bf16[96,4888]{1,0:T(8,128)(2,1)}) %all-reduce.19.cloned.1.call-update) | async-done | bytes 938512 | tf_op jit(solution)/shard_map/psum | solution.py:394
  651.1 16.7 %all-reduce.11 = f32[4,2834]{1,0:T(4,128)S(1)} all-reduce(f32[4,2834]{1,0:T(4,128)S(1)} %select_add_fusion), channel_id=9, replica_groups=mesh['section'=2,'group'=4,'replica'=4] {'group'}, use_global_device_ids=true, to_apply=%region_38.39.clone | all-reduce | flops 11336 | bytes 90688
  668.4 16.4 %psum.21 = f32[2834]{0:T(1024)S(1)} all-reduce(f32[2834]{0:T(1024)S(1)} %dynamic-slice_reduce_fusion), channel_id=1, replica_groups=mesh['section'=2,'group'=4,'replica'=4] {'replica'}, use_global_device_ids=true, to_apply=%region_39.40 | all-reduce | flops 2834 | bytes 22672 | tf_op jit(solution)/shard_map/psum | solution.py:485
  (705 shorter events, 171.0 us)
Async XLA Ops:
  7.2 79.4 %copy-start = (s32[2,1,8]{2,1,0:T(1,128)S(1)}, s32[2,1,8]{2,1,0:T(1,128)}, u32[]{:S(2)}) copy-start(s32[2,1,8]{2,1,0:T(1,128)} %param.14) | copy-start | bytes 196
  7.2 61.7 %all-gather.16.cloned.1.call-start = ((), (), s32[]{:S(2)}) async-start(), calls=%async_computation.4 | async-start | bytes 4792320 | tf_op jit(solution)/shard_map/all_gather | solution.py:423
  10.8 3.0 collective-permute-start.1
  11.3 57.7 %copy-start.199 = (bf16[1,448,4]{1,2,0:T(4,128)(2,1)S(1)}, bf16[1,448,4]{1,2,0:T(4,128)(2,1)}, u32[]{:S(2)}) copy-start(bf16[1,448,4]{1,2,0:T(4,128)(2,1)} %param.17) | copy-start | bytes 10756
  11.3 58.0 %copy-start.210 = (bf16[1,192]{1,0:T(2,128)(2,1)S(1)}, bf16[1,192]{1,0:T(2,128)(2,1)}, u32[]{:S(2)}) copy-start(bf16[1,192]{1,0:T(2,128)(2,1)} %param.15) | copy-start | bytes 1156
  11.3 58.1 %copy-start.208 = (bf16[1,448]{1,0:T(2,128)(2,1)S(1)}, bf16[1,448]{1,0:T(2,128)(2,1)}, u32[]{:S(2)}) copy-start(bf16[1,448]{1,0:T(2,128)(2,1)} %param.18) | copy-start | bytes 2692
  11.3 58.1 %copy-start.209 = (bf16[1,384]{1,0:T(2,128)(2,1)S(1)}, bf16[1,384]{1,0:T(2,128)(2,1)}, u32[]{:S(2)}) copy-start(bf16[1,384]{1,0:T(2,128)(2,1)} %param.22) | copy-start | bytes 2308
  11.3 58.1 %copy-start.204 = (u32[32]{0:T(128)S(1)}, u32[32]{0:T(128)}, u32[]{:S(2)}) copy-start(u32[32]{0:T(128)} %constant.154) | copy-start | bytes 388
  11.3 59.4 %copy-start.211 = (bf16[1,6]{1,0:T(2,128)(2,1)S(1)}, bf16[1,6]{1,0:T(2,128)(2,1)}, u32[]{:S(2)}) copy-start(bf16[1,6]{1,0:T(2,128)(2,1)} %param.19) | copy-start | bytes 40
  11.3 59.4 %copy-start.212 = (bf16[1,6]{1,0:T(2,128)(2,1)S(1)}, bf16[1,6]{1,0:T(2,128)(2,1)}, u32[]{:S(2)}) copy-start(bf16[1,6]{1,0:T(2,128)(2,1)} %param.20) | copy-start | bytes 40
  11.3 59.4 %copy-start.213 = (bf16[1,6]{1,0:T(2,128)(2,1)S(1)}, bf16[1,6]{1,0:T(2,128)(2,1)}, u32[]{:S(2)}) copy-start(bf16[1,6]{1,0:T(2,128)(2,1)} %param.21) | copy-start | bytes 40
  11.3 75.5 %copy-start.89 = (bf16[2,256,768]{2,1,0:T(8,128)(2,1)S(1)}, bf16[2,256,768]{2,1,0:T(8,128)(2,1)}, u32[]{:S(2)}) copy-start(bf16[2,256,768]{2,1,0:T(8,128)(2,1)} %param.12) | copy-start | bytes 2359300
  16.5 125.2 %all-gather.20.cloned.1.call-start = ((), (), s32[]{:S(2)}) async-start(), calls=%async_computation.6 | async-start | bytes 4792320 | tf_op jit(solution)/shard_map/all_gather | solution.py:426
  68.9 26.5 %collective-permute-start.2 = (bf16[4,96,4888]{2,1,0:T(8,128)(2,1)}, bf16[4,96,4888]{2,1,0:T(8,128)(2,1)}, u32[]{:S(2)}, u32[]{:S(2)}) collective-permute-start(bf16[4,96,4888]{2,1,0:T(8,128)(2,1)} %bitcast.394), channel_id=1, source_target_pairs={{0,16},{16,0},{1,17},{17,1},{2,18},{18,2},{3,19},{19,3},{4,20},{20... | collective-permute-start | bytes 11261960 | tf_op jit(solution)/shard_map/ppermute | solution.py:29
  86.5 4.1 collective-permute-start
  87.7 58.3 %copy-start.170 = (f32[256]{0:T(256)}, f32[256]{0:T(256)S(1)}, u32[]{:S(2)}) copy-start(f32[256]{0:T(256)S(1)} %add_rsqrt_fusion.3) | copy-start | bytes 3076
  89.1 21.1 %copy-start.166 = (f32[256]{0:T(256)}, f32[256]{0:T(256)S(1)}, u32[]{:S(2)}) copy-start(f32[256]{0:T(256)S(1)} %get-tuple-element.206) | copy-start | bytes 3076
  89.1 26.3 %copy-start.152 = (f32[256]{0:T(256)}, f32[256]{0:T(256)S(1)}, u32[]{:S(2)}) copy-start(f32[256]{0:T(256)S(1)} %get-tuple-element.208) | copy-start | bytes 3076
  89.1 54.9 %copy-start.187 = (f32[256]{0:T(256)}, f32[256]{0:T(256)S(1)}, u32[]{:S(2)}) copy-start(f32[256]{0:T(256)S(1)} %get-tuple-element.205) | copy-start | bytes 3076
  89.1 125.4 %copy-start.146 = (f32[256]{0:T(256)}, f32[256]{0:T(256)S(1)}, u32[]{:S(2)}) copy-start(f32[256]{0:T(256)S(1)} %get-tuple-element.204) | copy-start | bytes 3076
  89.1 125.4 %copy-start.149 = (f32[256]{0:T(256)}, f32[256]{0:T(256)S(1)}, u32[]{:S(2)}) copy-start(f32[256]{0:T(256)S(1)} %get-tuple-element.207) | copy-start | bytes 3076
  91.7 51.4 %copy-start.178 = (f32[24]{0:T(128)}, f32[24]{0:T(128)S(1)}, u32[]{:S(2)}) copy-start(f32[24]{0:T(128)S(1)} %reshape.799) | copy-start | bytes 292
  91.7 89.2 %all-gather.18.cloned.1.call-start = ((), (), s32[]{:S(2)}) async-start(), calls=%async_computation.5 | async-start | bytes 1966080 | tf_op jit(solution)/shard_map/all_gather | solution.py:216
  94.7 20.7 %copy-start.124 = (f32[1792]{0:T(1024)}, f32[1792]{0:T(1024)S(1)}, u32[]{:S(2)}) copy-start(f32[1792]{0:T(1024)S(1)} %get-tuple-element.105) | copy-start | bytes 21508
  94.7 20.7 %copy-start.126 = (f32[1792]{0:T(1024)}, f32[1792]{0:T(1024)S(1)}, u32[]{:S(2)}) copy-start(f32[1792]{0:T(1024)S(1)} %get-tuple-element.106) | copy-start | bytes 21508
  94.7 20.7 %copy-start.128 = (f32[1792]{0:T(1024)}, f32[1792]{0:T(1024)S(1)}, u32[]{:S(2)}) copy-start(f32[1792]{0:T(1024)S(1)} %get-tuple-element.107) | copy-start | bytes 21508
  94.7 20.7 %copy-start.130 = (f32[1792]{0:T(1024)}, f32[1792]{0:T(1024)S(1)}, u32[]{:S(2)}) copy-start(f32[1792]{0:T(1024)S(1)} %get-tuple-element.108) | copy-start | bytes 21508
  106.3 9.0 %collective-permute-start.3 = (f32[3,1792]{1,0:T(4,128)S(1)}, f32[3,1792]{1,0:T(4,128)S(1)}, u32[]{:S(2)}, u32[]{:S(2)}) collective-permute-start(f32[3,1792]{1,0:T(4,128)S(1)} %copy.223), channel_id=1, source_target_pairs={{0,1},{1,2},{2,3},{4,5},{5,6},{6,7},{8,9},{9,10},{10,11},{12,13},{... | collective-permute-start | bytes 64520 | tf_op jit(solution)/shard_map/ppermute | solution.py:25
  120.8 138.7 %all-gather.22.cloned.1.call-start = ((), (), s32[]{:S(2)}) async-start(), calls=%async_computation.7 | async-start | bytes 1966080 | tf_op jit(solution)/shard_map/all_gather | solution.py:216
  121.4 64.6 %copy-start.140 = (f32[1536]{0:T(1024)}, f32[1536]{0:T(1024)S(1)}, u32[]{:S(2)}) copy-start(f32[1536]{0:T(1024)S(1)} %mul.1221) | copy-start | bytes 18436
  121.4 66.5 %copy-start.99 = (f32[1536]{0:T(1024)}, f32[1536]{0:T(1024)S(1)}, u32[]{:S(2)}) copy-start(f32[1536]{0:T(1024)S(1)} %reshape.804) | copy-start | bytes 18436
  126.6 87.8 %copy-start.132 = (f32[1792]{0:T(1024)}, f32[1792]{0:T(1024)S(1)}, u32[]{:S(2)}) copy-start(f32[1792]{0:T(1024)S(1)} %get-tuple-element.101) | copy-start | bytes 21508
  126.6 87.8 %copy-start.134 = (f32[1792]{0:T(1024)}, f32[1792]{0:T(1024)S(1)}, u32[]{:S(2)}) copy-start(f32[1792]{0:T(1024)S(1)} %get-tuple-element.102) | copy-start | bytes 21508
  126.6 87.8 %copy-start.136 = (f32[1792]{0:T(1024)}, f32[1792]{0:T(1024)S(1)}, u32[]{:S(2)}) copy-start(f32[1792]{0:T(1024)S(1)} %get-tuple-element.103) | copy-start | bytes 21508
  126.6 87.8 %copy-start.138 = (f32[1792]{0:T(1024)}, f32[1792]{0:T(1024)S(1)}, u32[]{:S(2)}) copy-start(f32[1792]{0:T(1024)S(1)} %get-tuple-element.104) | copy-start | bytes 21508
  141.6 48.9 %collective-permute-start.4 = (bf16[4,96,4888]{2,1,0:T(8,128)(2,1)}, bf16[4,96,4888]{2,1,0:T(8,128)(2,1)}, u32[]{:S(2)}, u32[]{:S(2)}) collective-permute-start(bf16[4,96,4888]{2,1,0:T(8,128)(2,1)} %bitcast.392), channel_id=1, source_target_pairs={{0,16},{16,0},{1,17},{17,1},{2,18},{18,2},{3,19},{19,3},{4,20},{20... | collective-permute-start | bytes 11261960 | tf_op jit(solution)/shard_map/ppermute | solution.py:29
  142.8 38.1 %copy-start.106 = (f32[1536]{0:T(1024)}, f32[1536]{0:T(1024)S(1)}, u32[]{:S(2)}) copy-start(f32[1536]{0:T(1024)S(1)} %mul.1243) | copy-start | bytes 18436
  143.0 37.9 %copy-start.108 = (f32[1536]{0:T(1024)}, f32[1536]{0:T(1024)S(1)}, u32[]{:S(2)}) copy-start(f32[1536]{0:T(1024)S(1)} %mul.1239) | copy-start | bytes 18436
  143.1 37.8 %copy-start.110 = (f32[1536]{0:T(1024)}, f32[1536]{0:T(1024)S(1)}, u32[]{:S(2)}) copy-start(f32[1536]{0:T(1024)S(1)} %mul.1231) | copy-start | bytes 18436
  203.3 11.1 %collective-permute-start.5 = (f32[3,1792]{1,0:T(4,128)S(1)}, f32[3,1792]{1,0:T(4,128)S(1)}, u32[]{:S(2)}, u32[]{:S(2)}) collective-permute-start(f32[3,1792]{1,0:T(4,128)S(1)} %copy.225), channel_id=1, source_target_pairs={{0,1},{1,2},{2,3},{4,5},{5,6},{6,7},{8,9},{9,10},{10,11},{12,13},{... | collective-permute-start | bytes 64520 | tf_op jit(solution)/shard_map/ppermute | solution.py:25
  220.9 26.8 %copy-start.2 = (f32[256,1536]{1,0:T(8,128)}, f32[256,1536]{1,0:T(8,128)S(1)}, u32[]{:S(2)}) copy-start(f32[256,1536]{1,0:T(8,128)S(1)} %get-tuple-element.175.x_ref) | copy-start | bytes 4718596
  223.3 87.6 %all-gather.24.cloned.1.call-start = ((), (), s32[]{:S(2)}) async-start(), calls=%async_computation.8 | async-start | bytes 1966080 | tf_op jit(solution)/shard_map/all_gather | solution.py:216
  238.9 20.6 %copy-start.112 = (f32[1536]{0:T(1024)}, f32[1536]{0:T(1024)S(1)}, u32[]{:S(2)}) copy-start(f32[1536]{0:T(1024)S(1)} %mul.1299) | copy-start | bytes 18436
  274.7 143.1 %all-gather.26.cloned.1.call-start = ((), (), s32[]{:S(2)}) async-start(), calls=%async_computation.9 | async-start | bytes 1966080 | tf_op jit(solution)/shard_map/all_gather | solution.py:216
  334.7 6.2 collective-permute-start.7
  364.6 14.4 %collective-permute-start.11 = (bf16[4,96,4888]{2,1,0:T(8,128)(2,1)}, bf16[4,96,4888]{2,1,0:T(8,128)(2,1)}, u32[]{:S(2)}, u32[]{:S(2)}) collective-permute-start(bf16[4,96,4888]{2,1,0:T(8,128)(2,1)} %dynamic-slice_bitcast_fusion.1), channel_id=1, source_target_pairs={{0,16},{16,0},{1,17},{17,1},{2,18},{18,2},{3,19},{19,3},{4,20},{20... | collective-permute-start | bytes 11261960 | tf_op jit(solution)/shard_map/ppermute | solution.py:29
  378.9 90.6 %reduce-scatter.7.cloned.1.call-start = ((), (), s32[]{:S(2)}) async-start(), calls=%async_computation.10 | async-start | bytes 4792320
  385.0 136.5 %all-reduce.17.cloned.1.call-start = ((), (), s32[]{:S(2)}) async-start(), calls=%async_computation.2 | async-start | bytes 1916928 | tf_op jit(solution)/shard_map/psum | solution.py:394
  385.7 32.2 %copy-start.118 = (f32[1536]{0:T(1024)}, f32[1536]{0:T(1024)S(1)}, u32[]{:S(2)}) copy-start(f32[1536]{0:T(1024)S(1)} %mul.1412) | copy-start | bytes 18436
  385.9 32.0 %copy-start.120 = (f32[1536]{0:T(1024)}, f32[1536]{0:T(1024)S(1)}, u32[]{:S(2)}) copy-start(f32[1536]{0:T(1024)S(1)} %mul.1407) | copy-start | bytes 18436
  387.8 30.0 %copy-start.122 = (f32[1536]{0:T(1024)}, f32[1536]{0:T(1024)S(1)}, u32[]{:S(2)}) copy-start(f32[1536]{0:T(1024)S(1)} %mul.1402) | copy-start | bytes 18436
  436.5 33.1 %collective-permute-start.8 = (f32[3,1792]{1,0:T(4,128)S(1)}, f32[3,1792]{1,0:T(4,128)S(1)}, u32[]{:S(2)}, u32[]{:S(2)}) collective-permute-start(f32[3,1792]{1,0:T(4,128)S(1)} %pad_add_fusion.2), channel_id=1, source_target_pairs={{1,0},{2,1},{3,2},{5,4},{6,5},{7,6},{9,8},{10,9},{11,10},{13,12},{... | collective-permute-start | bytes 64520 | tf_op jit(solution)/shard_map/ppermute | solution.py:25
  469.6 127.2 %reduce-scatter.9.cloned.1.call-start = ((), (), s32[]{:S(2)}) async-start(), calls=%async_computation.11 | async-start | bytes 4792320
  471.3 50.1 %copy-start.171 = (f32[256]{0:T(256)S(1)}, f32[256]{0:T(256)}, u32[]{:S(2)}) copy-start(f32[256]{0:T(256)} %copy-done.170) | copy-start | bytes 3076
  538.0 6.7 collective-permute-start.12
  547.6 101.1 %all-reduce.19.cloned.1.call-start = ((), (), s32[]{:S(2)}) async-start(), calls=%async_computation.3 | async-start | bytes 1916928 | tf_op jit(solution)/shard_map/psum | solution.py:394
  552.3 2.0 collective-permute-start.6
  558.4 38.4 %copy-start.47 = (f32[256,768]{1,0:T(8,128)S(1)}, f32[256,768]{1,0:T(8,128)}, u32[]{:S(2)}) copy-start(f32[256,768]{1,0:T(8,128)} %copy-done.46) | copy-start | bytes 2359300
  596.8 51.9 %copy-start.77 = (bf16[96,4888]{1,0:T(8,128)(2,1)S(1)}, bf16[96,4888]{1,0:T(8,128)(2,1)}, u32[]{:S(2)}) copy-start(bf16[96,4888]{1,0:T(8,128)(2,1)} %all-reduce.17.cloned.1.call-done) | copy-start | bytes 2815492
  599.2 90.7 %collective-permute-start.9 = (f32[256,768]{1,0:T(8,128)}, f32[256,768]{1,0:T(8,128)}, u32[]{:S(2)}, u32[]{:S(2)}) collective-permute-start(f32[256,768]{1,0:T(8,128)} %fusion.123), channel_id=1, source_target_pairs={{0,16},{16,0},{1,17},{17,1},{2,18},{18,2},{3,19},{19,3},{4,20},{20... | collective-permute-start | bytes 2359304 | tf_op jit(solution)/shard_map/ppermute | solution.py:29
  599.5 90.5 %copy-start.88 = (f32[256,768]{1,0:T(8,128)S(1)}, f32[256,768]{1,0:T(8,128)}, u32[]{:S(2)}) copy-start(f32[256,768]{1,0:T(8,128)} %get-tuple-element.228) | copy-start | bytes 2359300
  599.5 90.5 %copy-start.92 = (bf16[2,256,768]{2,1,0:T(8,128)(2,1)S(1)}, bf16[2,256,768]{2,1,0:T(8,128)(2,1)}, u32[]{:S(2)}) copy-start(bf16[2,256,768]{2,1,0:T(8,128)(2,1)} %param.12) | copy-start | bytes 2359300
  599.5 51.5 %collective-permute-start.10 = (f32[4,2834]{1,0:T(4,128)S(1)}, f32[4,2834]{1,0:T(4,128)S(1)}, u32[]{:S(2)}, u32[]{:S(2)}) collective-permute-start(f32[4,2834]{1,0:T(4,128)S(1)} %broadcast_select_fusion.4), channel_id=1, source_target_pairs={{0,16},{16,0},{1,17},{17,1},{2,18},{18,2},{3,19},{19,3},{4,20},{20... | collective-permute-start | bytes 136040 | tf_op jit(solution)/shard_map/ppermute | solution.py:29
  649.8 42.9 %collective-permute-start.13 = (bf16[96,4888]{1,0:T(8,128)(2,1)}, bf16[96,4888]{1,0:T(8,128)(2,1)}, u32[]{:S(2)}, u32[]{:S(2)}) collective-permute-start(bf16[96,4888]{1,0:T(8,128)(2,1)} %broadcast_select_fusion), channel_id=1, source_target_pairs={{0,16},{16,0},{1,17},{17,1},{2,18},{18,2},{3,19},{19,3},{4,20},{20... | collective-permute-start | bytes 2815496 | tf_op jit(solution)/shard_map/ppermute | solution.py:29
  (179 other events, 591.2 us)
Sparse Core Ops, SparseCore 0:
  16.6 52.3 all-gather.15
  91.8 49.7 all-gather.19
  143.8 37.0 all-gather.17
  223.4 36.0 all-gather.21
  274.9 35.9 all-gather.23
  379.0 38.7 all-gather.25
  420.9 48.6 reduce-scatter.6
  472.0 49.4 all-reduce.16
  547.7 49.0 reduce-scatter.8
  599.1 49.4 all-reduce.18
